TPU v7x, 32 devices: a whole 2x2x4 slice. The times are simulated.
32 devices in a mesh: board: 8 (over y, x, core), hand: 4 (over z).
Axes of the slice: x: 2, y: 2, z: 4, core: 2. Of those that a mesh axis runs over, the one named last changes fastest.
Arguments:
- reach_pre: float32 [1408], P(('board', 'hand')), may hold values from 0.05 to 1
- strategy: bfloat16 [64, 128, 1408], P('board', None, 'hand'), may hold values from 0 to 1
- ranks: int32 [64, 8, 1408], P('board'), may hold values from 0 to 94
- boards: int32 [64, 8, 5], P('board'), may hold values from 0 to 51, as said below
- river_live: int32 [64], P('board'), may hold values from 1 to 8, as said below
- iso_weight: int32 [64], P('board'), may hold values from 1 to 24
- pot: float32 [128], replicated, may hold values from 2 to 24
- line_act: int32 [128], replicated, may hold values from 0 to 2
Outputs:
- preflop_value: float32 [1408], P('hand')
Inputs may be any that keep to these rules, and one draw needn't show every extreme that they name: `boards`: the five cards of a runout are distinct; all runouts of a flop share their first three cards. `river_live`: in every draw some flop has all 8 runouts live.
All inputs are finite; a program needn't handle non-finite values.
Results may differ from a plain program's by a relative error of at most 0.0003.
Values may be sent and summed in bfloat16 or wider, within the bound.
No kernel may reach another device: no remote copies, remote signals or barrier semaphores. Data moves between devices by JAX's collectives and lax.ppermute only.
A program may use at most 64 MiB of HBM per device.

v0:
```python
import functools

import jax
import jax.numpy as jnp
import numpy as np
from jax import lax
from jax.experimental import pallas as pl
from jax.experimental.pallas import tpu as pltpu
from jax.sharding import PartitionSpec as P

HANDS = 1326
HPAD = 1408
ACTS = 3
CARDS = 64
DEAD_CARD = 52
GROUP = 4
SPLITS = 3
PART = 4
FAR = 40
FAR_FLOPS = 24
RANKS = 128
USED_RANKS = 96
NO_RANK = 127.0

VMEM = pl.BlockSpec(memory_space=pltpu.VMEM)
SMEM = pl.BlockSpec(memory_space=pltpu.SMEM)
ANY = pl.BlockSpec(memory_space=pltpu.HBM)
NT = (((1,), (1,)), ((), ()))
TN = (((0,), (0,)), ((), ()))
EXACT = jnp.float8_e4m3fn


def hand_cards():
    first_card, second_card = np.triu_indices(52, 1)
    padding = HPAD - HANDS
    first_card = np.concatenate([first_card, np.full(padding, 52)])
    second_card = np.concatenate([second_card, np.full(padding, 53)])
    return jnp.asarray(np.stack([first_card, second_card]), jnp.int32)


def params(megabytes, flops=0, moved=10**6):
    return dict(
        compiler_params=pltpu.CompilerParams(vmem_limit_bytes=megabytes << 20),
        cost_estimate=pl.CostEstimate(flops=flops, bytes_accessed=moved, transcendentals=0),
    )


def copies_kernel(reach_ref, send_ref):
    send_ref[...] = jnp.broadcast_to(reach_ref[...], send_ref.shape)


def reach_copies(devices, reach):
    per = reach.shape[0]
    return pl.pallas_call(
        copies_kernel,
        out_shape=jax.ShapeDtypeStruct((devices, per), jnp.float32),
        in_specs=[VMEM],
        out_specs=VMEM,
        name="reach_copies",
        **params(1, 10**10, 10**8),
    )(reach.reshape(1, per))


def level(width):
    return lax.broadcasted_iota(jnp.int32, (USED_RANKS, width), 0).astype(jnp.float32)


def add_flops(first, last, count_ref, rank_rows, own_rows, live_rows, clear, holds, signs, sums_ref, sent):
    slots, rows = clear.shape
    runouts = holds.shape[0] // RANKS
    for low in range(0, runouts * RANKS, RANKS):
        holds[low + USED_RANKS : low + RANKS, :] = jnp.zeros((RANKS - USED_RANKS, slots), EXACT)
        signs[low + USED_RANKS : low + RANKS, :] = jnp.zeros((RANKS - USED_RANKS, rows), EXACT)

    def add_runout(at, low):
        span = pl.ds(pl.multiple_of(low, RANKS), USED_RANKS)
        rank = rank_rows[pl.ds(at, 1), :]
        holds[span, :] = jnp.where(rank == level(slots), 1.0, 0.0).astype(EXACT)
        sign = jnp.minimum(jnp.maximum(own_rows[pl.ds(at, 1), :] - level(rows), -1.0), 1.0)
        signs[span, :] = (sign * live_rows[pl.ds(at, 1), :]).astype(EXACT)

    def multiply(flop, depth):
        right = signs[:depth, :]
        for lane in range(0, slots, 256):
            part = slice(lane, min(lane + 256, slots))
            sign = lax.dot_general(holds[:depth, part], right, TN, preferred_element_type=jnp.float32)
            sums_ref[flop, part, :] = sign.astype(jnp.bfloat16) * clear[part, :]

    def one_flop(flop, carry):
        count = count_ref[flop]

        def one_runout(runout, carry):
            add_runout(flop * runouts + runout, runout * RANKS)
            return carry

        lax.fori_loop(0, count, one_runout, 0)

        @pl.when((lax.rem(count, 2) == 1) & (count > 1))
        def _():
            span = pl.ds(pl.multiple_of(count * RANKS, RANKS), RANKS)
            holds[span, :] = jnp.zeros((RANKS, slots), EXACT)
            signs[span, :] = jnp.zeros((RANKS, rows), EXACT)

        @pl.when(count == 1)
        def _():
            multiply(flop, RANKS)

        for step in range(2, runouts + 1, 2):

            @pl.when((count == step) | ((count == step - 1) & (count > 1)))
            def _():
                multiply(flop, step * RANKS)

        sent(flop)
        return carry

    lax.fori_loop(first, last, one_flop, 0)


def first_kernel(
    count_ref, ranks_ref, boards_ref, cards_ref, pot_ref, act_ref,
    far_ref, rank_rows, own_rows, live_rows, clear, weights_ref, holds, signs, sums, sem,
):
    slots, rows = clear.shape
    total = ranks_ref.shape[0]
    places, flops, runouts = boards_ref.shape
    start = lax.axis_index("hand") * rows
    turn = lax.rem(slots - start, slots)

    cards = cards_ref[...]
    own_cards = pltpu.roll(cards, turn, 1)[:, :rows]
    card = lax.broadcasted_iota(jnp.int32, (CARDS, slots), 0)
    holders = jnp.where((card == cards[0:1]) | (card == cards[1:2]), 1.0, 0.0).astype(EXACT)
    card = lax.broadcasted_iota(jnp.int32, (CARDS, rows), 0)
    own_holders = (card == own_cards[0:1]) | (card == own_cards[1:2])
    own_holders = jnp.where(own_holders, 1.0, 0.0).astype(EXACT)

    boards = jnp.concatenate([boards_ref[place] for place in range(places)], axis=1)
    row = lax.broadcasted_iota(jnp.int32, (total, flops), 0)
    of_flop = row // runouts == lax.broadcasted_iota(jnp.int32, (total, flops), 1)
    spread = jnp.dot(
        jnp.where(of_flop, 1.0, 0.0).astype(jnp.bfloat16),
        boards.astype(jnp.float32).astype(jnp.bfloat16),
        preferred_element_type=jnp.float32,
    )
    row = lax.broadcasted_iota(jnp.int32, spread.shape, 0)
    lane = lax.broadcasted_iota(jnp.int32, spread.shape, 1)
    mine = lax.rem(row, runouts) == lax.rem(lane, runouts)
    card = lax.broadcasted_iota(jnp.int32, (total, CARDS), 1)
    on_board = card == DEAD_CARD
    for place in range(places):
        here = mine & (lane // runouts == place)
        found = jnp.sum(jnp.where(here, spread, 0.0), axis=1, keepdims=True)
        on_board = on_board | (card.astype(jnp.float32) == found)
    on_board = jnp.where(on_board, 1.0, 0.0).astype(EXACT)

    hits = jnp.dot(on_board, holders, preferred_element_type=jnp.float32)
    ranks = jnp.where(hits > 0.0, NO_RANK, ranks_ref[...].astype(jnp.float32))
    rank_rows[...] = ranks
    own_ranks = pltpu.roll(ranks, turn, 1)[:, :rows]
    own_rows[...] = own_ranks
    live_rows[...] = jnp.where(own_ranks < NO_RANK, 1.0, 0.0)

    shared = lax.dot_general(holders, own_holders, TN, preferred_element_type=jnp.float32)
    clear[...] = jnp.maximum(1.0 - shared, 0.0).astype(jnp.bfloat16)

    act = act_ref[...]
    row = lax.broadcasted_iota(jnp.int32, (8, act.shape[1]), 0)
    weights = jnp.where(row == act, jnp.broadcast_to(pot_ref[...], row.shape), 0.0)
    weights_ref[...] = jnp.concatenate(split_bf16(weights), axis=0).astype(jnp.bfloat16)

    def copy(flop):
        return pltpu.make_async_copy(sums.at[flop], far_ref.at[flop], sem.at[flop])

    part = sums.shape[0]
    tables = (count_ref, rank_rows, own_rows, live_rows, clear, holds, signs)
    add_flops(0, part, *tables, sums, lambda flop: copy(flop).start())
    for flop in range(part):
        copy(flop).wait()


def showdown_scratch(runouts, slots, rows):
    return [
        pltpu.VMEM((runouts * RANKS, slots), EXACT),
        pltpu.VMEM((runouts * RANKS, rows), EXACT),
    ]


def first_flops(part, counts, ranks, boards, cards, pot, line_act, rows):
    total, slots = ranks.shape
    flops, lines = counts.shape[0], pot.shape[1]
    return pl.pallas_call(
        first_kernel,
        out_shape=[
            jax.ShapeDtypeStruct((FAR_FLOPS, slots, rows), jnp.bfloat16),
            jax.ShapeDtypeStruct((total, slots), jnp.float32),
            jax.ShapeDtypeStruct((total, rows), jnp.float32),
            jax.ShapeDtypeStruct((total, rows), jnp.float32),
            jax.ShapeDtypeStruct((slots, rows), jnp.bfloat16),
            jax.ShapeDtypeStruct((8 * SPLITS, lines), jnp.bfloat16),
        ],
        in_specs=[SMEM] + [VMEM] * 5,
        out_specs=[ANY] + [VMEM] * 5,
        scratch_shapes=showdown_scratch(total // flops, slots, rows)
        + [pltpu.VMEM((part, slots, rows), jnp.bfloat16), pltpu.SemaphoreType.DMA((part,))],
        name="first_flops",
        **params(FAR, 2 * 10**9, 10**7),
    )(counts, ranks, boards, cards, pot, line_act)


def other_kernel(
    part, count_ref, rank_rows, own_rows, live_rows, clear, grouped_ref, far_ref, sums_ref,
    holds, signs, sem,
):
    copies = [
        pltpu.make_async_copy(far_ref.at[flop], sums_ref.at[flop], sem.at[flop])
        for flop in range(part)
    ]
    for copy in copies:
        copy.start()
    tables = (count_ref, rank_rows, own_rows, live_rows, clear, holds, signs)
    add_flops(part, sums_ref.shape[0], *tables, sums_ref, lambda flop: None)
    for copy in copies:
        copy.wait()


def other_flops(part, counts, rank_rows, own_rows, live_rows, clear, grouped, far):
    slots, rows = clear.shape
    flops = counts.shape[0]
    return pl.pallas_call(
        functools.partial(other_kernel, part),
        out_shape=jax.ShapeDtypeStruct((flops, slots, rows), jnp.bfloat16),
        in_specs=[SMEM, VMEM, VMEM, VMEM, VMEM, ANY, ANY],
        out_specs=VMEM,
        scratch_shapes=showdown_scratch(rank_rows.shape[0] // flops, slots, rows)
        + [pltpu.SemaphoreType.DMA((part,))],
        name="other_flops",
        **params(FAR, 2 * 10**9, 10**7),
    )(counts, rank_rows, own_rows, live_rows, clear, grouped, far)


def split_bf16(values):
    parts = []
    for _ in range(SPLITS):
        part = values.astype(jnp.bfloat16).astype(jnp.float32)
        parts.append(part)
        values = values - part
    return parts


def action_kernel(reach_ref, strategy_ref, weights_ref, out_ref):
    flops, rows, lines = strategy_ref.shape
    senders, per = reach_ref.shape
    own = rows // per
    reach = reach_ref[...]
    slot = lax.broadcasted_iota(jnp.int32, (senders, per), 0) * per + lax.broadcasted_iota(
        jnp.int32, (senders, per), 1
    )
    alive = jnp.where(slot < HANDS, reach, 0.0)
    total = jnp.sum(jnp.sum(alive, axis=1, keepdims=True), axis=0, keepdims=True)

    mine = reach_ref[pl.ds(pl.multiple_of(lax.axis_index("hand") * own, 8), own), :]
    row = lax.broadcasted_iota(jnp.int32, (rows, own), 0)
    low = lax.broadcasted_iota(jnp.int32, (rows, own), 1) * per
    sender = jnp.where((row >= low) & (row < low + per), 1.0, 0.0)
    wide = jnp.dot(
        sender, mine, precision=lax.Precision.HIGHEST, preferred_element_type=jnp.float32
    )
    row = lax.broadcasted_iota(jnp.int32, (rows, per), 0)
    lane = lax.broadcasted_iota(jnp.int32, (rows, per), 1)
    own_reach = jnp.sum(jnp.where(lax.rem(row, per) == lane, wide, 0.0), axis=1, keepdims=True)
    scale = jnp.broadcast_to(own_reach / total, (rows, lines))

    weights = weights_ref[...]
    for flop in range(flops):
        line_reach = (strategy_ref[flop].astype(jnp.float32) * scale).astype(jnp.bfloat16)
        parts = lax.dot_general(weights, line_reach, NT, preferred_element_type=jnp.float32)
        sums = parts[0:8] + parts[8:16] + parts[16:24]
        out_ref[flop * GROUP : (flop + 1) * GROUP, :] = sums[0:GROUP]


def action_sums(reach, strategy, weights):
    flops, rows, lines = strategy.shape
    return pl.pallas_call(
        action_kernel,
        out_shape=jax.ShapeDtypeStruct((flops * GROUP, rows), jnp.float32),
        in_specs=[VMEM] * 3,
        out_specs=VMEM,
        name="action_sums",
        **params(4, 10**8),
    )(reach, strategy, weights)


def response_kernel(count_ref, weight_ref, sums_ref, *refs):
    shards, out_ref = refs[:-1], refs[-1]
    flops, slots, rows = sums_ref.shape
    gathered = jnp.zeros((flops * GROUP, slots), jnp.float32)
    for step, shard in enumerate(shards):
        at = jnp.bitwise_xor(lax.axis_index("hand"), step) * rows
        empty = jnp.zeros((flops * GROUP, slots - rows), jnp.float32)
        gathered = gathered + pltpu.roll(jnp.concatenate([shard[...], empty], axis=1), at, 1)
    splits = split_bf16(gathered)
    values = jnp.zeros((1, rows), jnp.float32)
    weight_sum = 0
    for flop in range(flops):
        low = flop * GROUP // 8 * 8
        left = jnp.concatenate([part[low : low + 8] for part in splits], axis=0)
        parts = jnp.dot(
            left.astype(jnp.bfloat16), sums_ref[flop], preferred_element_type=jnp.float32
        )
        group = parts[0:8] + parts[8:16] + parts[16:24]
        at = flop * GROUP - low
        best = jnp.max(group[at : at + ACTS], axis=0, keepdims=True)
        weight = weight_ref[flop]
        count = jnp.full((1, rows), count_ref[flop].astype(jnp.float32))
        values = values + best * weight.astype(jnp.float32) / count
        weight_sum = weight_sum + weight
    tail = jnp.full((1, out_ref.shape[1] - rows), weight_sum.astype(jnp.float32))
    out_ref[...] = jnp.broadcast_to(jnp.concatenate([values, tail], axis=1), out_ref.shape)


def best_response(counts, weights, sums, shards, copies):
    rows = sums.shape[2]
    width = -(-(rows + 1) // 128) * 128
    return pl.pallas_call(
        response_kernel,
        out_shape=jax.ShapeDtypeStruct((copies, width), jnp.float32),
        in_specs=[SMEM, SMEM] + [VMEM] * (1 + len(shards)),
        out_specs=VMEM,
        name="best_response",
        **params(12, 10**9, 10**7),
    )(counts, weights, sums, *shards)


def finish_kernel(parts_ref, out_ref):
    rows = out_ref.shape[0]
    whole = jnp.sum(parts_ref[...], axis=0)
    weight = whole[rows : rows + 1]
    out_ref[...] = whole[:rows] / weight


def finish(parts, rows):
    return pl.pallas_call(
        finish_kernel,
        out_shape=jax.ShapeDtypeStruct((rows,), jnp.float32),
        in_specs=[VMEM],
        out_specs=VMEM,
        name="finish",
        **params(2),
    )(parts)


def body(boards_n, hands_n, reach_pre, strategy, ranks, boards, river_live, iso_weight, pot, line_act):
    lines, rows = strategy.shape[1:]
    flops, runouts, slots = ranks.shape
    part = PART

    send = reach_copies(boards_n * hands_n, reach_pre)
    reach = lax.all_to_all(send, ("board", "hand"), 0, 0, tiled=True)
    far, *near, weights = first_flops(
        part,
        river_live,
        ranks.reshape(flops * runouts, slots),
        jnp.transpose(boards, (2, 0, 1)),
        hand_cards(),
        pot.reshape(1, lines),
        line_act.reshape(1, lines),
        rows,
    )

    grouped = action_sums(reach, jnp.swapaxes(strategy, 1, 2), weights)
    shards = [grouped]
    for step in range(1, hands_n):
        swap = [(source, source ^ step) for source in range(hands_n)]
        shards.append(lax.ppermute(grouped, "hand", swap))
    sums = other_flops(part, river_live, *near, grouped, far)

    partial = best_response(river_live, iso_weight, sums, shards, boards_n)
    return finish(lax.all_to_all(partial, "board", 0, 0, tiled=True), rows)


def solution(mesh):
    in_specs = (
        P(("board", "hand")),
        P("board", None, "hand"),
        P("board", None, None),
        P("board", None, None),
        P("board"),
        P("board"),
        P(),
        P(),
    )
    run = functools.partial(body, mesh.shape["board"], mesh.shape["hand"])
    return jax.shard_map(run, mesh=mesh, in_specs=in_specs, out_specs=P("hand"), check_vma=False)
```

profile of v0, /device:TPU:0, one launch (start us, length us, event | category | flops | bytes accessed | tf_op | source)
XLA Modules:
  0.0 34.6 jit_solution(3330946977388707820)
XLA Ops:
  0.0 0.0 copy-start.5
  0.0 0.7 %copy-done.5 = f32[44]{0:T(128)S(1)} copy-done((f32[44]{0:T(128)S(1)}, f32[44]{0:T(128)}, u32[]{:S(2)}) %copy-start.5) | copy-done | bytes 200
  0.7 0.0 copy-start.1
  0.7 0.0 copy-start.3
  0.7 0.0 copy-start.4
  0.7 0.0 copy-start.6
  0.7 0.0 copy-start.7
  0.7 0.0 copy-start.8
  0.7 0.0 copy-start
  0.7 0.6 %reach_copies.1 = f32[32,44]{1,0:T(8,128)} custom-call(f32[1,44]{1,0:T(1,128)S(1)} %bitcast.20), custom_call_target="tpu_custom_call" | custom-call | flops 10000000000 | bytes 100000000 | tf_op jit(solution)/shard_map/reach_copies/pallas_call | solution.py:54
  1.3 7.3 %all-to-all-start = ((f32[32,1,44]{2,1,0:T(1,128)}), f32[32,1,44]{2,1,0:T(1,128)S(1)}, u32[]{:S(2)}, u32[]{:S(2)}) async-start(f32[32,1,44]{2,1,0:T(1,128)} %bitcast.6), calls=%async_computation | async-start | bytes 32768 | tf_op jit(solution)/shard_map/all_to_all | solution.py:359
  8.6 0.0 copy-done.1
  8.6 0.0 copy-done.3
  8.6 0.0 copy-done.4
  8.6 0.0 copy-done.6
  8.6 0.0 copy-done.7
  8.7 0.0 copy-done.8
  8.7 4.5 %first_flops.1 = (bf16[24,1408,352]{2,1,0:T(8,128)(2,1)}, f32[64,1408]{1,0:T(8,128)S(1)}, f32[64,352]{1,0:T(8,128)S(1)}, f32[64,352]{1,0:T(8,128)S(1)}, bf16[140...) custom-call(s32[8]{0:T(128)S(1)} %copy-done.1, s32[64,1408]{1,0:T(8,128)S(1)} %bitcast.18, s32[5,8,8]{2,1,0:T(8,128)S(1)} %bitcast.19, ...), custom_call_target="tpu_custom_call" | custom-call | flops 2000000000 | bytes 10000000 | tf_op jit(solution)/shard_map/first_flops/pallas_call | solution.py:192
  13.2 2.6 %all-to-all-done = f32[32,1,44]{2,1,0:T(1,128)S(1)} async-done(((f32[32,1,44]{2,1,0:T(1,128)}), f32[32,1,44]{2,1,0:T(1,128)S(1)}, u32[]{:S(2)}, u32[]{:S(2)}) %all-to-all-start) | async-done | bytes 5664 | tf_op jit(solution)/shard_map/all_to_all | solution.py:359
  15.8 0.0 copy-done
  15.8 0.9 %action_sums.1.grouped_ref.refs_0_ = f32[32,352]{1,0:T(8,128)S(1)} custom-call(f32[32,44]{1,0:T(8,128)S(1)} %bitcast.15, bf16[8,352,128]{2,1,0:T(8,128)(2,1)S(1)} %bitcast.14, bf16[24,128]{1,0:T(8,128)(2,1)S(1)} %get-tuple-element.15.weights_ref), custom_call_target="tpu_custom_call" | custom-call | flops 100000000 | bytes 1000000 | tf_op jit(solution)/shard_map/action_sums/pallas_call | solution.py:284
  16.7 1.1 %collective-permute-start.2 = (f32[32,352]{1,0:T(8,128)S(1)}, f32[32,352]{1,0:T(8,128)S(1)}, u32[]{:S(2)}, u32[]{:S(2)}) collective-permute-start(f32[32,352]{1,0:T(8,128)S(1)} %action_sums.1.grouped_ref.refs_0_), channel_id=1, source_target_pairs={{0,3},{1,2},{2,1},{3,0},{4,7},{5,6},{6,5},{7,4},{8,11},{9,10},{10,... | collective-permute-start | bytes 135176 | tf_op jit(solution)/shard_map/ppermute | solution.py:375
  17.8 0.9 %collective-permute-start.1 = (f32[32,352]{1,0:T(8,128)S(1)}, f32[32,352]{1,0:T(8,128)S(1)}, u32[]{:S(2)}, u32[]{:S(2)}) collective-permute-start(f32[32,352]{1,0:T(8,128)S(1)} %action_sums.1.grouped_ref.refs_0_), channel_id=1, source_target_pairs={{0,2},{1,3},{2,0},{3,1},{4,6},{5,7},{6,4},{7,5},{8,10},{9,11},{10,... | collective-permute-start | bytes 135176 | tf_op jit(solution)/shard_map/ppermute | solution.py:375
  18.7 2.4 %collective-permute-start = (f32[32,352]{1,0:T(8,128)S(1)}, f32[32,352]{1,0:T(8,128)S(1)}, u32[]{:S(2)}, u32[]{:S(2)}) collective-permute-start(f32[32,352]{1,0:T(8,128)S(1)} %action_sums.1.grouped_ref.refs_0_), channel_id=1, source_target_pairs={{0,1},{1,0},{2,3},{3,2},{4,5},{5,4},{6,7},{7,6},{8,9},{9,8},{10,11... | collective-permute-start | bytes 135176 | tf_op jit(solution)/shard_map/ppermute | solution.py:375
  21.2 3.5 %other_flops.1.sums_ref = bf16[8,1408,352]{2,1,0:T(8,128)(2,1)S(1)} custom-call(s32[8]{0:T(128)S(1)} %copy-done.1, f32[64,1408]{1,0:T(8,128)S(1)} %get-tuple-element.11.rank_rows, f32[64,352]{1,0:T(8,128)S(1)} %get-tuple-element.12.own_rows, f32[64,352]{1,0:T(8,128)S(1)} %get-tuple-element.13.live_rows, bf16[1408,352]{1,0:T(8,128)(2,1)S(1)} %get-tuple-element.14.clear, ...), custom_call_target="tpu_custom_call" | custom-call | flops 2000000000 | bytes 10000000 | tf_op jit(solution)/shard_map/other_flops/pallas_call | solution.py:230
  24.7 0.0 collective-permute-done.2.refs_3_
  24.7 0.0 collective-permute-done.1.refs_2_
  24.7 0.0 collective-permute-done.refs_1_
  24.7 0.0 copy-done.2
  24.7 2.1 %best_response.1 = f32[8,384]{1,0:T(8,128)S(1)} custom-call(s32[8]{0:T(128)S(1)} %copy-done.1, s32[8]{0:T(128)S(1)} %copy-done.2, bf16[8,1408,352]{2,1,0:T(8,128)(2,1)S(1)} %other_flops.1.sums_ref, f32[32,352]{1,0:T(8,128)S(1)} %action_sums.1.grouped_ref.refs_0_, f32[32,352]{1,0:T(8,128)S(1)} %collective-permute-done.refs_1_, ...), custom_call_target="tpu_custom_call" | custom-call | flops 1000000000 | bytes 10000000 | tf_op jit(solution)/shard_map/best_response/pallas_call | solution.py:325
  26.8 7.2 %all_to_all.22 = f32[8,1,384]{2,1,0:T(1,128)S(1)} all-to-all(f32[8,1,384]{2,1,0:T(1,128)S(1)} %copy.11), channel_id=1, replica_groups=mesh['board'=8,'hand'=4] {'board'}, dimensions={0} | all-to-all | bytes 24576 | tf_op jit(solution)/shard_map/all_to_all | solution.py:379
  34.0 0.7 %finish.1 = f32[352]{0:T(512)} custom-call(f32[8,384]{1,0:T(8,128)S(1)} %bitcast.17), custom_call_target="tpu_custom_call" | custom-call | bytes 1000000 | tf_op jit(solution)/shard_map/finish/pallas_call | solution.py:343
  (3 shorter events, 0.0 us)
Async XLA Ops:
  0.0 0.7 %copy-start.5 = (f32[44]{0:T(128)S(1)}, f32[44]{0:T(128)}, u32[]{:S(2)}) copy-start(f32[44]{0:T(128)} %param.9) | copy-start | bytes 532
  0.7 8.0 %copy-start.1 = (s32[8]{0:T(128)S(1)}, s32[8]{0:T(128)}, u32[]{:S(2)}) copy-start(s32[8]{0:T(128)} %count_ref.5) | copy-start | bytes 100
  0.7 8.0 %copy-start.3 = (s32[8,8,1408]{2,1,0:T(8,128)S(1)}, s32[8,8,1408]{2,1,0:T(8,128)}, u32[]{:S(2)}) copy-start(s32[8,8,1408]{2,1,0:T(8,128)} %param.11) | copy-start | bytes 1081348
  0.7 8.0 %copy-start.4 = (s32[8,8,5]{1,0,2:T(8,128)S(1)}, s32[8,8,5]{1,0,2:T(8,128)}, u32[]{:S(2)}) copy-start(s32[8,8,5]{1,0,2:T(8,128)} %param.12) | copy-start | bytes 3844
  0.7 8.0 %copy-start.6 = (f32[128]{0:T(128)S(1)}, f32[128]{0:T(128)}, u32[]{:S(2)}) copy-start(f32[128]{0:T(128)} %param.15) | copy-start | bytes 1540
  0.7 8.0 %copy-start.7 = (s32[128]{0:T(128)S(1)}, s32[128]{0:T(128)}, u32[]{:S(2)}) copy-start(s32[128]{0:T(128)} %param.16) | copy-start | bytes 1540
  0.7 8.0 %copy-start.8 = (s32[2,1408]{1,0:T(2,128)S(1)}, s32[2,1408]{1,0:T(2,128)}, u32[]{:S(2)}) copy-start(s32[2,1408]{1,0:T(2,128)} %constant.2.clone.cards_ref) | copy-start | bytes 33796
  0.7 15.1 %copy-start = (bf16[8,128,352]{1,2,0:T(8,128)(2,1)S(1)}, bf16[8,128,352]{1,2,0:T(8,128)(2,1)}, u32[]{:S(2)}) copy-start(bf16[8,128,352]{1,2,0:T(8,128)(2,1)} %param.10) | copy-start | bytes 2162692
  1.3 14.5 %all-to-all-start = ((f32[32,1,44]{2,1,0:T(1,128)}), f32[32,1,44]{2,1,0:T(1,128)S(1)}, u32[]{:S(2)}, u32[]{:S(2)}) async-start(f32[32,1,44]{2,1,0:T(1,128)} %bitcast.6), calls=%async_computation | async-start | bytes 32768 | tf_op jit(solution)/shard_map/all_to_all | solution.py:359
  16.7 8.0 %collective-permute-start.2 = (f32[32,352]{1,0:T(8,128)S(1)}, f32[32,352]{1,0:T(8,128)S(1)}, u32[]{:S(2)}, u32[]{:S(2)}) collective-permute-start(f32[32,352]{1,0:T(8,128)S(1)} %action_sums.1.grouped_ref.refs_0_), channel_id=1, source_target_pairs={{0,3},{1,2},{2,1},{3,0},{4,7},{5,6},{6,5},{7,4},{8,11},{9,10},{10,... | collective-permute-start | bytes 135176 | tf_op jit(solution)/shard_map/ppermute | solution.py:375
  17.8 6.9 %collective-permute-start.1 = (f32[32,352]{1,0:T(8,128)S(1)}, f32[32,352]{1,0:T(8,128)S(1)}, u32[]{:S(2)}, u32[]{:S(2)}) collective-permute-start(f32[32,352]{1,0:T(8,128)S(1)} %action_sums.1.grouped_ref.refs_0_), channel_id=1, source_target_pairs={{0,2},{1,3},{2,0},{3,1},{4,6},{5,7},{6,4},{7,5},{8,10},{9,11},{10,... | collective-permute-start | bytes 135176 | tf_op jit(solution)/shard_map/ppermute | solution.py:375
  18.7 6.0 %collective-permute-start = (f32[32,352]{1,0:T(8,128)S(1)}, f32[32,352]{1,0:T(8,128)S(1)}, u32[]{:S(2)}, u32[]{:S(2)}) collective-permute-start(f32[32,352]{1,0:T(8,128)S(1)} %action_sums.1.grouped_ref.refs_0_), channel_id=1, source_target_pairs={{0,1},{1,0},{2,3},{3,2},{4,5},{5,4},{6,7},{7,6},{8,9},{9,8},{10,11... | collective-permute-start | bytes 135176 | tf_op jit(solution)/shard_map/ppermute | solution.py:375
  21.2 3.5 %copy-start.2 = (s32[8]{0:T(128)S(1)}, s32[8]{0:T(128)}, u32[]{:S(2)}) copy-start(s32[8]{0:T(128)} %weight_ref.1) | copy-start | bytes 100
where the time goes:
time: 35 us; the launch traced here: 34.6 us
  Pallas kernels  12.2 us (35%)
  starting transfers between devices  11.7 us (33%)
  blocking collectives  7.18 us (21%)
  waiting for transfers between devices  2.63 us (8%)
  local copies, waits for them, and re-layouts  0.7 us (2%)
    all_to_all x1, starting transfers between devices, body(): reach = lax.all_to_all(send, ('board', 'hand'), 0, 0, tiled=True)  7.3 us
    all_to_all x1, blocking collectives, body(): return finish(lax.all_to_all(partial, 'board', 0, 0, tiled=True), rows)  7.18 us
    pallas_call x1, Pallas kernels, first_flops(): pl.pallas_call(first_kernel, out_shape=[jax.ShapeDtypeStruct((FAR_FLOPS,...  4.48 us
    ppermute x3, starting transfers between devices, body(): shards.append(lax.ppermute(grouped, 'hand', swap))  4.45 us
    pallas_call x1, Pallas kernels, other_flops(): pl.pallas_call(functools.partial(other_kernel, part), out_shape=jax.Shape...  3.5 us
    all_to_all x1, waiting for transfers between devices, body(): reach = lax.all_to_all(send, ('board', 'hand'), 0, 0, tiled=True)  2.63 us
    pallas_call x1, Pallas kernels, best_response(): pl.pallas_call(response_kernel, out_shape=jax.ShapeDtypeStruct((copies, w...  2.07 us
    pallas_call x1, Pallas kernels, action_sums(): pl.pallas_call(action_kernel, out_shape=jax.ShapeDtypeStruct((flops * GRO...  0.93 us
  transfers between devices with their start and end apart: 4, of which 1 were waited for; matrix products, arithmetic and copies ran while one was open for 0% of the time, Pallas kernels for 23%

commit v1 on v0

--- a/solution.py
+++ b/solution.py
@@ -65,7 +65,7 @@
     return lax.broadcasted_iota(jnp.int32, (USED_RANKS, width), 0).astype(jnp.float32)
 
 
-def add_flops(first, last, count_ref, rank_rows, own_rows, live_rows, clear, holds, signs, sums_ref, sent):
+def add_flops(first, last, count_ref, rank_rows, own_rows, clear, holds, signs, sums_ref, sent):
     slots, rows = clear.shape
     runouts = holds.shape[0] // RANKS
     for low in range(0, runouts * RANKS, RANKS):
@@ -76,8 +76,10 @@
         span = pl.ds(pl.multiple_of(low, RANKS), USED_RANKS)
         rank = rank_rows[pl.ds(at, 1), :]
         holds[span, :] = jnp.where(rank == level(slots), 1.0, 0.0).astype(EXACT)
-        sign = jnp.minimum(jnp.maximum(own_rows[pl.ds(at, 1), :] - level(rows), -1.0), 1.0)
-        signs[span, :] = (sign * live_rows[pl.ds(at, 1), :]).astype(EXACT)
+        rank = own_rows[pl.ds(at, 1), :]
+        live = jnp.where(rank < NO_RANK, 1.0, 0.0)
+        sign = jnp.minimum(jnp.maximum(rank - level(rows), -1.0), 1.0)
+        signs[span, :] = (sign * live).astype(EXACT)
 
     def multiply(flop, depth):
         right = signs[:depth, :]
@@ -90,7 +92,7 @@
         count = count_ref[flop]
 
         def one_runout(runout, carry):
-            add_runout(flop * runouts + runout, runout * RANKS)
+            add_runout((flop - first) * runouts + runout, runout * RANKS)
             return carry
 
         lax.fori_loop(0, count, one_runout, 0)
@@ -119,7 +121,8 @@
 
 def first_kernel(
     count_ref, ranks_ref, boards_ref, cards_ref, pot_ref, act_ref,
-    far_ref, rank_rows, own_rows, live_rows, clear, weights_ref, holds, signs, sums, sem,
+    far_ref, near_ref, late_ranks, late_own, clear, weights_ref,
+    holds, signs, rank_rows, own_rows, sums, sem,
 ):
     slots, rows = clear.shape
     total = ranks_ref.shape[0]
@@ -159,7 +162,8 @@
     rank_rows[...] = ranks
     own_ranks = pltpu.roll(ranks, turn, 1)[:, :rows]
     own_rows[...] = own_ranks
-    live_rows[...] = jnp.where(own_ranks < NO_RANK, 1.0, 0.0)
+    late_ranks[...] = ranks[total - late_ranks.shape[0] :]
+    late_own[...] = own_ranks[total - late_own.shape[0] :]
 
     shared = lax.dot_general(holders, own_holders, TN, preferred_element_type=jnp.float32)
     clear[...] = jnp.maximum(1.0 - shared, 0.0).astype(jnp.bfloat16)
@@ -172,10 +176,16 @@
     def copy(flop):
         return pltpu.make_async_copy(sums.at[flop], far_ref.at[flop], sem.at[flop])
 
-    part = sums.shape[0]
-    tables = (count_ref, rank_rows, own_rows, live_rows, clear, holds, signs)
-    add_flops(0, part, *tables, sums, lambda flop: copy(flop).start())
-    for flop in range(part):
+    def sent(flop):
+        @pl.when(flop < last)
+        def _():
+            copy(flop).start()
+
+    last = sums.shape[0] - 1
+    tables = (count_ref, rank_rows, own_rows, clear, holds, signs)
+    add_flops(0, last + 1, *tables, sums, sent)
+    near_ref[...] = sums[last]
+    for flop in range(last):
         copy(flop).wait()
 
 
@@ -189,54 +199,60 @@
 def first_flops(part, counts, ranks, boards, cards, pot, line_act, rows):
     total, slots = ranks.shape
     flops, lines = counts.shape[0], pot.shape[1]
+    late = total // flops * (flops - part)
     return pl.pallas_call(
         first_kernel,
         out_shape=[
             jax.ShapeDtypeStruct((FAR_FLOPS, slots, rows), jnp.bfloat16),
-            jax.ShapeDtypeStruct((total, slots), jnp.float32),
-            jax.ShapeDtypeStruct((total, rows), jnp.float32),
-            jax.ShapeDtypeStruct((total, rows), jnp.float32),
+            jax.ShapeDtypeStruct((slots, rows), jnp.bfloat16),
+            jax.ShapeDtypeStruct((late, slots), jnp.float32),
+            jax.ShapeDtypeStruct((late, rows), jnp.float32),
             jax.ShapeDtypeStruct((slots, rows), jnp.bfloat16),
             jax.ShapeDtypeStruct((8 * SPLITS, lines), jnp.bfloat16),
         ],
         in_specs=[SMEM] + [VMEM] * 5,
         out_specs=[ANY] + [VMEM] * 5,
         scratch_shapes=showdown_scratch(total // flops, slots, rows)
-        + [pltpu.VMEM((part, slots, rows), jnp.bfloat16), pltpu.SemaphoreType.DMA((part,))],
+        + [
+            pltpu.VMEM((total, slots), jnp.float32),
+            pltpu.VMEM((total, rows), jnp.float32),
+            pltpu.VMEM((part, slots, rows), jnp.bfloat16),
+            pltpu.SemaphoreType.DMA((part - 1,)),
+        ],
         name="first_flops",
         **params(FAR, 2 * 10**9, 10**7),
     )(counts, ranks, boards, cards, pot, line_act)
 
 
 def other_kernel(
-    part, count_ref, rank_rows, own_rows, live_rows, clear, grouped_ref, far_ref, sums_ref,
+    part, count_ref, rank_rows, own_rows, clear, grouped_ref, far_ref, sums_ref,
     holds, signs, sem,
 ):
     copies = [
         pltpu.make_async_copy(far_ref.at[flop], sums_ref.at[flop], sem.at[flop])
-        for flop in range(part)
+        for flop in range(part - 1)
     ]
     for copy in copies:
         copy.start()
-    tables = (count_ref, rank_rows, own_rows, live_rows, clear, holds, signs)
-    add_flops(part, sums_ref.shape[0], *tables, sums_ref, lambda flop: None)
+    tables = (count_ref, rank_rows, own_rows, clear, holds, signs)
+    add_flops(part, count_ref.shape[0], *tables, sums_ref, lambda flop: None)
     for copy in copies:
         copy.wait()
 
 
-def other_flops(part, counts, rank_rows, own_rows, live_rows, clear, grouped, far):
+def other_flops(part, counts, rank_rows, own_rows, clear, grouped, far):
     slots, rows = clear.shape
     flops = counts.shape[0]
     return pl.pallas_call(
         functools.partial(other_kernel, part),
         out_shape=jax.ShapeDtypeStruct((flops, slots, rows), jnp.bfloat16),
-        in_specs=[SMEM, VMEM, VMEM, VMEM, VMEM, ANY, ANY],
+        in_specs=[SMEM, VMEM, VMEM, VMEM, ANY, ANY],
         out_specs=VMEM,
-        scratch_shapes=showdown_scratch(rank_rows.shape[0] // flops, slots, rows)
-        + [pltpu.SemaphoreType.DMA((part,))],
+        scratch_shapes=showdown_scratch(rank_rows.shape[0] // (flops - part), slots, rows)
+        + [pltpu.SemaphoreType.DMA((part - 1,))],
         name="other_flops",
         **params(FAR, 2 * 10**9, 10**7),
-    )(counts, rank_rows, own_rows, live_rows, clear, grouped, far)
+    )(counts, rank_rows, own_rows, clear, grouped, far)
 
 
 def split_bf16(values):
@@ -260,12 +276,11 @@
     total = jnp.sum(jnp.sum(alive, axis=1, keepdims=True), axis=0, keepdims=True)
 
     mine = reach_ref[pl.ds(pl.multiple_of(lax.axis_index("hand") * own, 8), own), :]
-    row = lax.broadcasted_iota(jnp.int32, (rows, own), 0)
-    low = lax.broadcasted_iota(jnp.int32, (rows, own), 1) * per
-    sender = jnp.where((row >= low) & (row < low + per), 1.0, 0.0)
-    wide = jnp.dot(
-        sender, mine, precision=lax.Precision.HIGHEST, preferred_element_type=jnp.float32
-    )
+    mine = jnp.concatenate(split_bf16(mine), axis=0).astype(jnp.bfloat16)
+    row = lax.broadcasted_iota(jnp.int32, (rows, own * SPLITS), 0)
+    low = lax.rem(lax.broadcasted_iota(jnp.int32, (rows, own * SPLITS), 1), own) * per
+    sender = jnp.where((row >= low) & (row < low + per), 1.0, 0.0).astype(jnp.bfloat16)
+    wide = jnp.dot(sender, mine, preferred_element_type=jnp.float32)
     row = lax.broadcasted_iota(jnp.int32, (rows, per), 0)
     lane = lax.broadcasted_iota(jnp.int32, (rows, per), 1)
     own_reach = jnp.sum(jnp.where(lax.rem(row, per) == lane, wide, 0.0), axis=1, keepdims=True)
@@ -291,7 +306,7 @@
     )(reach, strategy, weights)
 
 
-def response_kernel(count_ref, weight_ref, sums_ref, *refs):
+def response_kernel(single, count_ref, weight_ref, sums_ref, near_ref, *refs):
     shards, out_ref = refs[:-1], refs[-1]
     flops, slots, rows = sums_ref.shape
     gathered = jnp.zeros((flops * GROUP, slots), jnp.float32)
@@ -303,10 +318,11 @@
     values = jnp.zeros((1, rows), jnp.float32)
     weight_sum = 0
     for flop in range(flops):
+        matrix = near_ref if flop == single else sums_ref.at[flop]
         low = flop * GROUP // 8 * 8
         left = jnp.concatenate([part[low : low + 8] for part in splits], axis=0)
         parts = jnp.dot(
-            left.astype(jnp.bfloat16), sums_ref[flop], preferred_element_type=jnp.float32
+            left.astype(jnp.bfloat16), matrix[...], preferred_element_type=jnp.float32
         )
         group = parts[0:8] + parts[8:16] + parts[16:24]
         at = flop * GROUP - low
@@ -319,17 +335,17 @@
     out_ref[...] = jnp.broadcast_to(jnp.concatenate([values, tail], axis=1), out_ref.shape)
 
 
-def best_response(counts, weights, sums, shards, copies):
+def best_response(single, counts, weights, sums, near, shards, copies):
     rows = sums.shape[2]
     width = -(-(rows + 1) // 128) * 128
     return pl.pallas_call(
-        response_kernel,
+        functools.partial(response_kernel, single),
         out_shape=jax.ShapeDtypeStruct((copies, width), jnp.float32),
-        in_specs=[SMEM, SMEM] + [VMEM] * (1 + len(shards)),
+        in_specs=[SMEM, SMEM] + [VMEM] * (2 + len(shards)),
         out_specs=VMEM,
         name="best_response",
         **params(12, 10**9, 10**7),
-    )(counts, weights, sums, *shards)
+    )(counts, weights, sums, near, *shards)
 
 
 def finish_kernel(parts_ref, out_ref):
@@ -357,7 +373,7 @@
 
     send = reach_copies(boards_n * hands_n, reach_pre)
     reach = lax.all_to_all(send, ("board", "hand"), 0, 0, tiled=True)
-    far, *near, weights = first_flops(
+    far, near, *tables, weights = first_flops(
         part,
         river_live,
         ranks.reshape(flops * runouts, slots),
@@ -373,9 +389,9 @@
     for step in range(1, hands_n):
         swap = [(source, source ^ step) for source in range(hands_n)]
         shards.append(lax.ppermute(grouped, "hand", swap))
-    sums = other_flops(part, river_live, *near, grouped, far)
-
-    partial = best_response(river_live, iso_weight, sums, shards, boards_n)
+    sums = other_flops(part, river_live, *tables, grouped, far)
+
+    partial = best_response(part - 1, river_live, iso_weight, sums, near, shards, boards_n)
     return finish(lax.all_to_all(partial, "board", 0, 0, tiled=True), rows)
 
 

time: 35 us -> 34.1 us (0.974)
  Pallas kernels: 12.2 us -> 10.4 us
  waiting for transfers between devices: 2.63 us -> 3.57 us
    pallas_call x1, Pallas kernels: 3.5 us -> 2.45 us  [other_flops(): pl.pallas_call(functools.partial(other_kernel, part), out_shape=jax.Shape...]
    all_to_all x1, waiting for transfers between devices: 2.63 us -> 3.11 us  [body(): reach = lax.all_to_all(send, ('board', 'hand'), 0, 0, tiled=True)]
    pallas_call x1, Pallas kernels: 4.48 us -> 3.99 us  [first_flops(): pl.pallas_call(first_kernel, out_shape=[jax.ShapeDtypeStruct((FAR_FLOPS,...]
    ppermute x3, waiting for transfers between devices: 0.01 us -> 0.46 us  [body(): shards.append(lax.ppermute(grouped, 'hand', swap))]
  transfers between devices with their start and end apart: 4 -> 4, of which waited for: 1 -> 2; matrix products, arithmetic and copies ran while one was open for 0% -> 0% of each run, Pallas kernels for 23% -> 19%
where the time goes in v1:
time: 34.1 us; the launch traced here: 34 us
  starting transfers between devices  11.8 us (35%)
  Pallas kernels  10.4 us (30%)
  blocking collectives  7.47 us (22%)
  waiting for transfers between devices  3.57 us (10%)
  local copies, waits for them, and re-layouts  0.7 us (2%)
    all_to_all x1, blocking collectives, body(): return finish(lax.all_to_all(partial, 'board', 0, 0, tiled=True), rows)  7.47 us
    all_to_all x1, starting transfers between devices, body(): reach = lax.all_to_all(send, ('board', 'hand'), 0, 0, tiled=True)  7.3 us
    ppermute x3, starting transfers between devices, body(): shards.append(lax.ppermute(grouped, 'hand', swap))  4.45 us
    pallas_call x1, Pallas kernels, first_flops(): pl.pallas_call(first_kernel, out_shape=[jax.ShapeDtypeStruct((FAR_FLOPS,...  3.99 us
    all_to_all x1, waiting for transfers between devices, body(): reach = lax.all_to_all(send, ('board', 'hand'), 0, 0, tiled=True)  3.11 us
    pallas_call x1, Pallas kernels, other_flops(): pl.pallas_call(functools.partial(other_kernel, part), out_shape=jax.Shape...  2.45 us
    pallas_call x1, Pallas kernels, best_response(): pl.pallas_call(functools.partial(response_kernel, single), out_shape=jax....  2.07 us
    unnamed x19, local copies, waits for them, and re-layouts  0.69 us
  transfers between devices with their start and end apart: 4, of which 2 were waited for; matrix products, arithmetic and copies ran while one was open for 0% of the time, Pallas kernels for 19%

profile of v1, /device:TPU:0, one launch (start us, length us, event | category | flops | bytes accessed | tf_op | source)
XLA Modules:
  0.0 34.0 jit_solution(6438269789609878700)
XLA Ops:
  0.0 0.0 copy-start.5
  0.0 0.7 %copy-done.5 = f32[44]{0:T(128)S(1)} copy-done((f32[44]{0:T(128)S(1)}, f32[44]{0:T(128)}, u32[]{:S(2)}) %copy-start.5) | copy-done | bytes 200
  0.7 0.0 copy-start.1
  0.7 0.0 copy-start.4
  0.7 0.0 copy-start.6
  0.7 0.0 copy-start.7
  0.7 0.0 copy-start.8
  0.7 0.0 copy-start
  0.7 0.6 %reach_copies.1 = f32[32,44]{1,0:T(8,128)} custom-call(f32[1,44]{1,0:T(1,128)S(1)} %bitcast.20), custom_call_target="tpu_custom_call" | custom-call | flops 10000000000 | bytes 100000000 | tf_op jit(solution)/shard_map/reach_copies/pallas_call | solution.py:54
  1.3 7.3 %all-to-all-start = ((f32[32,1,44]{2,1,0:T(1,128)}), f32[32,1,44]{2,1,0:T(1,128)S(1)}, u32[]{:S(2)}, u32[]{:S(2)}) async-start(f32[32,1,44]{2,1,0:T(1,128)} %bitcast.6), calls=%async_computation | async-start | bytes 32768 | tf_op jit(solution)/shard_map/all_to_all | solution.py:375
  8.6 0.0 copy-done.1
  8.6 0.0 copy-done.3
  8.6 0.0 copy-done.4
  8.6 0.0 copy-done.6
  8.6 0.0 copy-done.7
  8.7 0.0 copy-done.8
  8.7 4.0 %first_flops.1 = (bf16[24,1408,352]{2,1,0:T(8,128)(2,1)}, bf16[1408,352]{1,0:T(8,128)(2,1)S(1)}, f32[32,1408]{1,0:T(8,128)S(1)}, f32[32,352]{1,0:T(8,128)S(1)}, ...) custom-call(s32[8]{0:T(128)S(1)} %copy-done.1, s32[64,1408]{1,0:T(8,128)S(1)} %bitcast.18, ...), custom_call_target="tpu_custom_call" | custom-call | flops 2000000000 | bytes 10000000 | tf_op jit(solution)/shard_map/first_flops/pallas_call | solution.py:203
  12.7 3.1 %all-to-all-done = f32[32,1,44]{2,1,0:T(1,128)S(1)} async-done(((f32[32,1,44]{2,1,0:T(1,128)}), f32[32,1,44]{2,1,0:T(1,128)S(1)}, u32[]{:S(2)}, u32[]{:S(2)}) %all-to-all-start) | async-done | bytes 5664 | tf_op jit(solution)/shard_map/all_to_all | solution.py:375
  15.8 0.0 copy-done
  15.8 0.6 %action_sums.1.grouped_ref.refs_0_ = f32[32,352]{1,0:T(8,128)S(1)} custom-call(f32[32,44]{1,0:T(8,128)S(1)} %bitcast.15, bf16[8,352,128]{2,1,0:T(8,128)(2,1)S(1)} %bitcast.14, bf16[24,128]{1,0:T(8,128)(2,1)S(1)} %get-tuple-element.14.weights_ref), custom_call_target="tpu_custom_call" | custom-call | flops 100000000 | bytes 1000000 | tf_op jit(solution)/shard_map/action_sums/pallas_call | solution.py:299
  16.4 0.6 %collective-permute-start.2 = (f32[32,352]{1,0:T(8,128)S(1)}, f32[32,352]{1,0:T(8,128)S(1)}, u32[]{:S(2)}, u32[]{:S(2)}) collective-permute-start(f32[32,352]{1,0:T(8,128)S(1)} %action_sums.1.grouped_ref.refs_0_), channel_id=1, source_target_pairs={{0,3},{1,2},{2,1},{3,0},{4,7},{5,6},{6,5},{7,4},{8,11},{9,10},{10,... | collective-permute-start | bytes 135176 | tf_op jit(solution)/shard_map/ppermute | solution.py:391
  17.0 1.4 %collective-permute-start.1 = (f32[32,352]{1,0:T(8,128)S(1)}, f32[32,352]{1,0:T(8,128)S(1)}, u32[]{:S(2)}, u32[]{:S(2)}) collective-permute-start(f32[32,352]{1,0:T(8,128)S(1)} %action_sums.1.grouped_ref.refs_0_), channel_id=1, source_target_pairs={{0,2},{1,3},{2,0},{3,1},{4,6},{5,7},{6,4},{7,5},{8,10},{9,11},{10,... | collective-permute-start | bytes 135176 | tf_op jit(solution)/shard_map/ppermute | solution.py:391
  18.4 2.4 %collective-permute-start = (f32[32,352]{1,0:T(8,128)S(1)}, f32[32,352]{1,0:T(8,128)S(1)}, u32[]{:S(2)}, u32[]{:S(2)}) collective-permute-start(f32[32,352]{1,0:T(8,128)S(1)} %action_sums.1.grouped_ref.refs_0_), channel_id=1, source_target_pairs={{0,1},{1,0},{2,3},{3,2},{4,5},{5,4},{6,7},{7,6},{8,9},{9,8},{10,11... | collective-permute-start | bytes 135176 | tf_op jit(solution)/shard_map/ppermute | solution.py:391
  20.8 0.0 copy-start.2
  20.8 2.5 %other_flops.1.sums_ref = bf16[8,1408,352]{2,1,0:T(8,128)(2,1)S(1)} custom-call(s32[8]{0:T(128)S(1)} %copy-done.1, f32[32,1408]{1,0:T(8,128)S(1)} %get-tuple-element.11.rank_rows, f32[32,352]{1,0:T(8,128)S(1)} %get-tuple-element.12.own_rows, bf16[1408,352]{1,0:T(8,128)(2,1)S(1)} %get-tuple-element.13.clear, f32[32,352]{1,0:T(8,128)S(1)} %action_sums.1.grouped_ref.refs_0_, ...), custom_call_target="tpu_custom_call" | custom-call | flops 2000000000 | bytes 10000000 | tf_op jit(solution)/shard_map/other_flops/pallas_call | solution.py:246
  23.3 0.0 collective-permute-done.2.refs_3_
  23.3 0.5 %collective-permute-done.1.refs_2_ = f32[32,352]{1,0:T(8,128)S(1)} collective-permute-done((f32[32,352]{1,0:T(8,128)S(1)}, f32[32,352]{1,0:T(8,128)S(1)}, u32[]{:S(2)}, u32[]{:S(2)}) %collective-permute-start.1) | collective-permute-done | bytes 45088 | tf_op jit(solution)/shard_map/ppermute | solution.py:391
  23.8 0.0 collective-permute-done.refs_1_
  23.8 0.0 copy-done.2
  23.8 2.1 %best_response.1 = f32[8,384]{1,0:T(8,128)S(1)} custom-call(s32[8]{0:T(128)S(1)} %copy-done.1, s32[8]{0:T(128)S(1)} %copy-done.2, bf16[8,1408,352]{2,1,0:T(8,128)(2,1)S(1)} %other_flops.1.sums_ref, bf16[1408,352]{1,0:T(8,128)(2,1)S(1)} %get-tuple-element.16.near_ref, f32[32,352]{1,0:T(8,128)S(1)} %action_sums.1.grouped_ref.refs_0_, ...), custom_call_target="tpu_custom_call" | custom-call | flops 1000000000 | bytes 10000000 | tf_op jit(solution)/shard_map/best_response/pallas_call | solution.py:341
  25.9 7.5 %all_to_all.22 = f32[8,1,384]{2,1,0:T(1,128)S(1)} all-to-all(f32[8,1,384]{2,1,0:T(1,128)S(1)} %copy.11), channel_id=1, replica_groups=mesh['board'=8,'hand'=4] {'board'}, dimensions={0} | all-to-all | bytes 24576 | tf_op jit(solution)/shard_map/all_to_all | solution.py:395
  33.3 0.7 %finish.1 = f32[352]{0:T(512)} custom-call(f32[8,384]{1,0:T(8,128)S(1)} %bitcast.16), custom_call_target="tpu_custom_call" | custom-call | bytes 1000000 | tf_op jit(solution)/shard_map/finish/pallas_call | solution.py:359
  (3 shorter events, 0.0 us)
Async XLA Ops:
  0.0 0.7 %copy-start.5 = (f32[44]{0:T(128)S(1)}, f32[44]{0:T(128)}, u32[]{:S(2)}) copy-start(f32[44]{0:T(128)} %param.9) | copy-start | bytes 532
  0.7 8.0 %copy-start.1 = (s32[8]{0:T(128)S(1)}, s32[8]{0:T(128)}, u32[]{:S(2)}) copy-start(s32[8]{0:T(128)} %count_ref.5) | copy-start | bytes 100
  0.7 8.0 %copy-start.3 = (s32[8,8,1408]{2,1,0:T(8,128)S(1)}, s32[8,8,1408]{2,1,0:T(8,128)}, u32[]{:S(2)}) copy-start(s32[8,8,1408]{2,1,0:T(8,128)} %param.11) | copy-start | bytes 1081348
  0.7 8.0 %copy-start.4 = (s32[8,8,5]{1,0,2:T(8,128)S(1)}, s32[8,8,5]{1,0,2:T(8,128)}, u32[]{:S(2)}) copy-start(s32[8,8,5]{1,0,2:T(8,128)} %param.12) | copy-start | bytes 3844
  0.7 8.0 %copy-start.6 = (f32[128]{0:T(128)S(1)}, f32[128]{0:T(128)}, u32[]{:S(2)}) copy-start(f32[128]{0:T(128)} %param.15) | copy-start | bytes 1540
  0.7 8.0 %copy-start.7 = (s32[128]{0:T(128)S(1)}, s32[128]{0:T(128)}, u32[]{:S(2)}) copy-start(s32[128]{0:T(128)} %param.16) | copy-start | bytes 1540
  0.7 8.0 %copy-start.8 = (s32[2,1408]{1,0:T(2,128)S(1)}, s32[2,1408]{1,0:T(2,128)}, u32[]{:S(2)}) copy-start(s32[2,1408]{1,0:T(2,128)} %constant.2.clone.cards_ref) | copy-start | bytes 33796
  0.7 15.1 %copy-start = (bf16[8,128,352]{1,2,0:T(8,128)(2,1)S(1)}, bf16[8,128,352]{1,2,0:T(8,128)(2,1)}, u32[]{:S(2)}) copy-start(bf16[8,128,352]{1,2,0:T(8,128)(2,1)} %param.10) | copy-start | bytes 2162692
  1.3 14.5 %all-to-all-start = ((f32[32,1,44]{2,1,0:T(1,128)}), f32[32,1,44]{2,1,0:T(1,128)S(1)}, u32[]{:S(2)}, u32[]{:S(2)}) async-start(f32[32,1,44]{2,1,0:T(1,128)} %bitcast.6), calls=%async_computation | async-start | bytes 32768 | tf_op jit(solution)/shard_map/all_to_all | solution.py:375
  16.4 6.9 %collective-permute-start.2 = (f32[32,352]{1,0:T(8,128)S(1)}, f32[32,352]{1,0:T(8,128)S(1)}, u32[]{:S(2)}, u32[]{:S(2)}) collective-permute-start(f32[32,352]{1,0:T(8,128)S(1)} %action_sums.1.grouped_ref.refs_0_), channel_id=1, source_target_pairs={{0,3},{1,2},{2,1},{3,0},{4,7},{5,6},{6,5},{7,4},{8,11},{9,10},{10,... | collective-permute-start | bytes 135176 | tf_op jit(solution)/shard_map/ppermute | solution.py:391
  17.0 6.8 %collective-permute-start.1 = (f32[32,352]{1,0:T(8,128)S(1)}, f32[32,352]{1,0:T(8,128)S(1)}, u32[]{:S(2)}, u32[]{:S(2)}) collective-permute-start(f32[32,352]{1,0:T(8,128)S(1)} %action_sums.1.grouped_ref.refs_0_), channel_id=1, source_target_pairs={{0,2},{1,3},{2,0},{3,1},{4,6},{5,7},{6,4},{7,5},{8,10},{9,11},{10,... | collective-permute-start | bytes 135176 | tf_op jit(solution)/shard_map/ppermute | solution.py:391
  18.4 5.4 %collective-permute-start = (f32[32,352]{1,0:T(8,128)S(1)}, f32[32,352]{1,0:T(8,128)S(1)}, u32[]{:S(2)}, u32[]{:S(2)}) collective-permute-start(f32[32,352]{1,0:T(8,128)S(1)} %action_sums.1.grouped_ref.refs_0_), channel_id=1, source_target_pairs={{0,1},{1,0},{2,3},{3,2},{4,5},{5,4},{6,7},{7,6},{8,9},{9,8},{10,11... | collective-permute-start | bytes 135176 | tf_op jit(solution)/shard_map/ppermute | solution.py:391
  20.8 2.9 %copy-start.2 = (s32[8]{0:T(128)S(1)}, s32[8]{0:T(128)}, u32[]{:S(2)}) copy-start(s32[8]{0:T(128)} %weight_ref.1) | copy-start | bytes 100

commit v2 on v1

--- a/solution.py
+++ b/solution.py
@@ -23,7 +23,6 @@
 NO_RANK = 127.0
 
 VMEM = pl.BlockSpec(memory_space=pltpu.VMEM)
-SMEM = pl.BlockSpec(memory_space=pltpu.SMEM)
 ANY = pl.BlockSpec(memory_space=pltpu.HBM)
 NT = (((1,), (1,)), ((), ()))
 TN = (((0,), (0,)), ((), ()))
@@ -65,17 +64,23 @@
     return lax.broadcasted_iota(jnp.int32, (USED_RANKS, width), 0).astype(jnp.float32)
 
 
-def add_flops(first, last, count_ref, rank_rows, own_rows, clear, holds, signs, sums_ref, sent):
+def add_flops(first, last, counts, rank_rows, own_rows, clear, holds, signs, sums_ref, sent):
     slots, rows = clear.shape
     runouts = holds.shape[0] // RANKS
     for low in range(0, runouts * RANKS, RANKS):
         holds[low + USED_RANKS : low + RANKS, :] = jnp.zeros((RANKS - USED_RANKS, slots), EXACT)
         signs[low + USED_RANKS : low + RANKS, :] = jnp.zeros((RANKS - USED_RANKS, rows), EXACT)
 
+    one, zero = jnp.ones((32, slots), EXACT), jnp.zeros((32, slots), EXACT)
+    down = lax.broadcasted_iota(jnp.int32, one.shape, 0)
+
     def add_runout(at, low):
         span = pl.ds(pl.multiple_of(low, RANKS), USED_RANKS)
-        rank = rank_rows[pl.ds(at, 1), :]
-        holds[span, :] = jnp.where(rank == level(slots), 1.0, 0.0).astype(EXACT)
+        rank = jnp.broadcast_to(rank_rows[pl.ds(at, 1), :].astype(jnp.int32), one.shape)
+        rank = rank.astype(jnp.int8)
+        for step in range(0, USED_RANKS, one.shape[0]):
+            held = jnp.where(rank == (down + step).astype(jnp.int8), one, zero)
+            holds[pl.ds(pl.multiple_of(low + step, one.shape[0]), one.shape[0]), :] = held
         rank = own_rows[pl.ds(at, 1), :]
         live = jnp.where(rank < NO_RANK, 1.0, 0.0)
         sign = jnp.minimum(jnp.maximum(rank - level(rows), -1.0), 1.0)
@@ -89,7 +94,7 @@
             sums_ref[flop, part, :] = sign.astype(jnp.bfloat16) * clear[part, :]
 
     def one_flop(flop, carry):
-        count = count_ref[flop]
+        count = counts[flop]
 
         def one_runout(runout, carry):
             add_runout((flop - first) * runouts + runout, runout * RANKS)
@@ -122,8 +127,9 @@
 def first_kernel(
     count_ref, ranks_ref, boards_ref, cards_ref, pot_ref, act_ref,
     far_ref, near_ref, late_ranks, late_own, clear, weights_ref,
-    holds, signs, rank_rows, own_rows, sums, sem,
+    counts, holds, signs, rank_rows, own_rows, sums, sem,
 ):
+    read_counts(count_ref, counts)
     slots, rows = clear.shape
     total = ranks_ref.shape[0]
     places, flops, runouts = boards_ref.shape
@@ -182,15 +188,21 @@
             copy(flop).start()
 
     last = sums.shape[0] - 1
-    tables = (count_ref, rank_rows, own_rows, clear, holds, signs)
+    tables = (counts, rank_rows, own_rows, clear, holds, signs)
     add_flops(0, last + 1, *tables, sums, sent)
     near_ref[...] = sums[last]
     for flop in range(last):
         copy(flop).wait()
 
 
-def showdown_scratch(runouts, slots, rows):
+def read_counts(count_ref, counts):
+    for flop in range(count_ref.shape[1]):
+        counts[flop] = count_ref[0, flop]
+
+
+def showdown_scratch(flops, runouts, slots, rows):
     return [
+        pltpu.SMEM((flops,), jnp.int32),
         pltpu.VMEM((runouts * RANKS, slots), EXACT),
         pltpu.VMEM((runouts * RANKS, rows), EXACT),
     ]
@@ -198,7 +210,7 @@
 
 def first_flops(part, counts, ranks, boards, cards, pot, line_act, rows):
     total, slots = ranks.shape
-    flops, lines = counts.shape[0], pot.shape[1]
+    flops, lines = counts.shape[1], pot.shape[1]
     late = total // flops * (flops - part)
     return pl.pallas_call(
         first_kernel,
@@ -210,9 +222,9 @@
             jax.ShapeDtypeStruct((slots, rows), jnp.bfloat16),
             jax.ShapeDtypeStruct((8 * SPLITS, lines), jnp.bfloat16),
         ],
-        in_specs=[SMEM] + [VMEM] * 5,
+        in_specs=[VMEM] * 6,
         out_specs=[ANY] + [VMEM] * 5,
-        scratch_shapes=showdown_scratch(total // flops, slots, rows)
+        scratch_shapes=showdown_scratch(flops, total // flops, slots, rows)
         + [
             pltpu.VMEM((total, slots), jnp.float32),
             pltpu.VMEM((total, rows), jnp.float32),
@@ -226,29 +238,30 @@
 
 def other_kernel(
     part, count_ref, rank_rows, own_rows, clear, grouped_ref, far_ref, sums_ref,
-    holds, signs, sem,
+    counts, holds, signs, sem,
 ):
+    read_counts(count_ref, counts)
     copies = [
         pltpu.make_async_copy(far_ref.at[flop], sums_ref.at[flop], sem.at[flop])
         for flop in range(part - 1)
     ]
     for copy in copies:
         copy.start()
-    tables = (count_ref, rank_rows, own_rows, clear, holds, signs)
-    add_flops(part, count_ref.shape[0], *tables, sums_ref, lambda flop: None)
+    tables = (counts, rank_rows, own_rows, clear, holds, signs)
+    add_flops(part, count_ref.shape[1], *tables, sums_ref, lambda flop: None)
     for copy in copies:
         copy.wait()
 
 
 def other_flops(part, counts, rank_rows, own_rows, clear, grouped, far):
     slots, rows = clear.shape
-    flops = counts.shape[0]
+    flops = counts.shape[1]
     return pl.pallas_call(
         functools.partial(other_kernel, part),
         out_shape=jax.ShapeDtypeStruct((flops, slots, rows), jnp.bfloat16),
-        in_specs=[SMEM, VMEM, VMEM, VMEM, ANY, ANY],
+        in_specs=[VMEM] * 4 + [ANY] * 2,
         out_specs=VMEM,
-        scratch_shapes=showdown_scratch(rank_rows.shape[0] // (flops - part), slots, rows)
+        scratch_shapes=showdown_scratch(flops, rank_rows.shape[0] // (flops - part), slots, rows)
         + [pltpu.SemaphoreType.DMA((part - 1,))],
         name="other_flops",
         **params(FAR, 2 * 10**9, 10**7),
@@ -307,7 +320,7 @@
 
 
 def response_kernel(single, count_ref, weight_ref, sums_ref, near_ref, *refs):
-    shards, out_ref = refs[:-1], refs[-1]
+    shards, out_ref, products = refs[:-2], refs[-2], refs[-1]
     flops, slots, rows = sums_ref.shape
     gathered = jnp.zeros((flops * GROUP, slots), jnp.float32)
     for step, shard in enumerate(shards):
@@ -315,23 +328,24 @@
         empty = jnp.zeros((flops * GROUP, slots - rows), jnp.float32)
         gathered = gathered + pltpu.roll(jnp.concatenate([shard[...], empty], axis=1), at, 1)
     splits = split_bf16(gathered)
-    values = jnp.zeros((1, rows), jnp.float32)
-    weight_sum = 0
     for flop in range(flops):
         matrix = near_ref if flop == single else sums_ref.at[flop]
         low = flop * GROUP // 8 * 8
         left = jnp.concatenate([part[low : low + 8] for part in splits], axis=0)
-        parts = jnp.dot(
+        products[flop] = jnp.dot(
             left.astype(jnp.bfloat16), matrix[...], preferred_element_type=jnp.float32
         )
-        group = parts[0:8] + parts[8:16] + parts[16:24]
-        at = flop * GROUP - low
+
+    values = jnp.zeros((1, rows), jnp.float32)
+    weights = weight_ref[...].astype(jnp.float32)
+    counts = count_ref[...].astype(jnp.float32)
+    for flop in range(flops):
+        group = products[flop, 0:8] + products[flop, 8:16] + products[flop, 16:24]
+        at = flop * GROUP % 8
         best = jnp.max(group[at : at + ACTS], axis=0, keepdims=True)
-        weight = weight_ref[flop]
-        count = jnp.full((1, rows), count_ref[flop].astype(jnp.float32))
-        values = values + best * weight.astype(jnp.float32) / count
-        weight_sum = weight_sum + weight
-    tail = jnp.full((1, out_ref.shape[1] - rows), weight_sum.astype(jnp.float32))
+        values = values + best * weights[:, flop : flop + 1] / counts[:, flop : flop + 1]
+    tail = jnp.sum(weights, axis=1, keepdims=True)
+    tail = jnp.broadcast_to(tail, (1, out_ref.shape[1] - rows))
     out_ref[...] = jnp.broadcast_to(jnp.concatenate([values, tail], axis=1), out_ref.shape)
 
 
@@ -341,8 +355,9 @@
     return pl.pallas_call(
         functools.partial(response_kernel, single),
         out_shape=jax.ShapeDtypeStruct((copies, width), jnp.float32),
-        in_specs=[SMEM, SMEM] + [VMEM] * (2 + len(shards)),
+        in_specs=[VMEM] * (4 + len(shards)),
         out_specs=VMEM,
+        scratch_shapes=[pltpu.VMEM((sums.shape[0], 8 * SPLITS, rows), jnp.float32)],
         name="best_response",
         **params(12, 10**9, 10**7),
     )(counts, weights, sums, near, *shards)
@@ -370,12 +385,13 @@
     lines, rows = strategy.shape[1:]
     flops, runouts, slots = ranks.shape
     part = PART
+    counts = river_live.reshape(1, flops)
 
     send = reach_copies(boards_n * hands_n, reach_pre)
     reach = lax.all_to_all(send, ("board", "hand"), 0, 0, tiled=True)
     far, near, *tables, weights = first_flops(
         part,
-        river_live,
+        counts,
         ranks.reshape(flops * runouts, slots),
         jnp.transpose(boards, (2, 0, 1)),
         hand_cards(),
@@ -389,9 +405,10 @@
     for step in range(1, hands_n):
         swap = [(source, source ^ step) for source in range(hands_n)]
         shards.append(lax.ppermute(grouped, "hand", swap))
-    sums = other_flops(part, river_live, *tables, grouped, far)
-
-    partial = best_response(part - 1, river_live, iso_weight, sums, near, shards, boards_n)
+    sums = other_flops(part, counts, *tables, grouped, far)
+
+    weights = iso_weight.reshape(1, flops)
+    partial = best_response(part - 1, counts, weights, sums, near, shards, boards_n)
     return finish(lax.all_to_all(partial, "board", 0, 0, tiled=True), rows)
 
 

time: 34.1 us -> 33.2 us (0.974)
  Pallas kernels: 10.4 us -> 9.9 us
  blocking collectives: 7.47 us -> 7.1 us
    pallas_call x1, Pallas kernels: 2.07 us -> 1.52 us  [best_response(): pl.pallas_call(functools.partial(response_kernel, single), out_shape=jax....]
    all_to_all x1, blocking collectives: 7.47 us -> 7.1 us  [body(): return finish(lax.all_to_all(partial, 'board', 0, 0, tiled=True), rows)]
  transfers between devices with their start and end apart: 4 -> 4, of which waited for: 2 -> 2; matrix products, arithmetic and copies ran while one was open for 0% -> 0% of each run, Pallas kernels for 19% -> 20%
where the time goes in v2:
time: 33.2 us; the launch traced here: 32.9 us
  starting transfers between devices  11.8 us (36%)
  Pallas kernels  9.9 us (30%)
  blocking collectives  7.1 us (21%)
  waiting for transfers between devices  3.33 us (10%)
  local copies, waits for them, and re-layouts  0.7 us (2%)
    all_to_all x1, starting transfers between devices, body(): reach = lax.all_to_all(send, ('board', 'hand'), 0, 0, tiled=True)  7.3 us
    all_to_all x1, blocking collectives, body(): return finish(lax.all_to_all(partial, 'board', 0, 0, tiled=True), rows)  7.1 us
    ppermute x3, starting transfers between devices, body(): shards.append(lax.ppermute(grouped, 'hand', swap))  4.45 us
    pallas_call x1, Pallas kernels, first_flops(): pl.pallas_call(first_kernel, out_shape=[jax.ShapeDtypeStruct((FAR_FLOPS,...  4.05 us
    all_to_all x1, waiting for transfers between devices, body(): reach = lax.all_to_all(send, ('board', 'hand'), 0, 0, tiled=True)  3.05 us
    pallas_call x1, Pallas kernels, other_flops(): pl.pallas_call(functools.partial(other_kernel, part), out_shape=jax.Shape...  2.49 us
    pallas_call x1, Pallas kernels, best_response(): pl.pallas_call(functools.partial(response_kernel, single), out_shape=jax....  1.52 us
    unnamed x19, local copies, waits for them, and re-layouts  0.69 us
  transfers between devices with their start and end apart: 4, of which 2 were waited for; matrix products, arithmetic and copies ran while one was open for 0% of the time, Pallas kernels for 20%

profile of v2, /device:TPU:0, one launch (start us, length us, event | category | flops | bytes accessed | tf_op | source)
XLA Modules:
  0.0 32.9 jit_solution(12563483540480549271)
XLA Ops:
  0.0 0.0 copy-start.5
  0.0 0.7 %copy-done.5 = f32[44]{0:T(128)S(1)} copy-done((f32[44]{0:T(128)S(1)}, f32[44]{0:T(128)}, u32[]{:S(2)}) %copy-start.5) | copy-done | bytes 200
  0.7 0.0 copy-start.1
  0.7 0.0 copy-start.3
  0.7 0.0 copy-start.4
  0.7 0.0 copy-start.6
  0.7 0.0 copy-start.7
  0.7 0.0 copy-start.8
  0.7 0.0 copy-start
  0.7 0.6 %reach_copies.1 = f32[32,44]{1,0:T(8,128)} custom-call(f32[1,44]{1,0:T(1,128)S(1)} %bitcast.26), custom_call_target="tpu_custom_call" | custom-call | flops 10000000000 | bytes 100000000 | tf_op jit(solution)/shard_map/reach_copies/pallas_call | solution.py:53
  1.3 7.3 %all-to-all-start = ((f32[32,1,44]{2,1,0:T(1,128)}), f32[32,1,44]{2,1,0:T(1,128)S(1)}, u32[]{:S(2)}, u32[]{:S(2)}) async-start(f32[32,1,44]{2,1,0:T(1,128)} %bitcast.8), calls=%async_computation | async-start | bytes 32768 | tf_op jit(solution)/shard_map/all_to_all | solution.py:391
  8.6 0.0 copy-done.1
  8.6 0.0 copy-done.3
  8.6 0.0 copy-done.4
  8.6 0.0 copy-done.6
  8.6 0.0 copy-done.7
  8.7 0.0 copy-done.8
  8.7 4.1 %first_flops.1 = (bf16[24,1408,352]{2,1,0:T(8,128)(2,1)}, bf16[1408,352]{1,0:T(8,128)(2,1)S(1)}, f32[32,1408]{1,0:T(8,128)S(1)}, f32[32,352]{1,0:T(8,128)S(1)}, ...) custom-call(s32[1,8]{1,0:T(1,128)S(1)} %bitcast.20, s32[64,1408]{1,0:T(8,128)S(1)} %bitcast.24, ...), custom_call_target="tpu_custom_call" | custom-call | flops 2000000000 | bytes 10000000 | tf_op jit(solution)/shard_map/first_flops/pallas_call | solution.py:215
  12.7 3.1 %all-to-all-done = f32[32,1,44]{2,1,0:T(1,128)S(1)} async-done(((f32[32,1,44]{2,1,0:T(1,128)}), f32[32,1,44]{2,1,0:T(1,128)S(1)}, u32[]{:S(2)}, u32[]{:S(2)}) %all-to-all-start) | async-done | bytes 5664 | tf_op jit(solution)/shard_map/all_to_all | solution.py:391
  15.8 0.0 copy-done
  15.8 0.6 %action_sums.1.grouped_ref.refs_0_ = f32[32,352]{1,0:T(8,128)S(1)} custom-call(f32[32,44]{1,0:T(8,128)S(1)} %bitcast.17, bf16[8,352,128]{2,1,0:T(8,128)(2,1)S(1)} %bitcast.16, bf16[24,128]{1,0:T(8,128)(2,1)S(1)} %get-tuple-element.14.weights_ref), custom_call_target="tpu_custom_call" | custom-call | flops 100000000 | bytes 1000000 | tf_op jit(solution)/shard_map/action_sums/pallas_call | solution.py:312
  16.4 0.7 %collective-permute-start.2 = (f32[32,352]{1,0:T(8,128)S(1)}, f32[32,352]{1,0:T(8,128)S(1)}, u32[]{:S(2)}, u32[]{:S(2)}) collective-permute-start(f32[32,352]{1,0:T(8,128)S(1)} %action_sums.1.grouped_ref.refs_0_), channel_id=1, source_target_pairs={{0,3},{1,2},{2,1},{3,0},{4,7},{5,6},{6,5},{7,4},{8,11},{9,10},{10,... | collective-permute-start | bytes 135176 | tf_op jit(solution)/shard_map/ppermute | solution.py:407
  17.0 1.4 %collective-permute-start.1 = (f32[32,352]{1,0:T(8,128)S(1)}, f32[32,352]{1,0:T(8,128)S(1)}, u32[]{:S(2)}, u32[]{:S(2)}) collective-permute-start(f32[32,352]{1,0:T(8,128)S(1)} %action_sums.1.grouped_ref.refs_0_), channel_id=1, source_target_pairs={{0,2},{1,3},{2,0},{3,1},{4,6},{5,7},{6,4},{7,5},{8,10},{9,11},{10,... | collective-permute-start | bytes 135176 | tf_op jit(solution)/shard_map/ppermute | solution.py:407
  18.4 2.4 %collective-permute-start = (f32[32,352]{1,0:T(8,128)S(1)}, f32[32,352]{1,0:T(8,128)S(1)}, u32[]{:S(2)}, u32[]{:S(2)}) collective-permute-start(f32[32,352]{1,0:T(8,128)S(1)} %action_sums.1.grouped_ref.refs_0_), channel_id=1, source_target_pairs={{0,1},{1,0},{2,3},{3,2},{4,5},{5,4},{6,7},{7,6},{8,9},{9,8},{10,11... | collective-permute-start | bytes 135176 | tf_op jit(solution)/shard_map/ppermute | solution.py:407
  20.8 2.5 %other_flops.1.sums_ref = bf16[8,1408,352]{2,1,0:T(8,128)(2,1)S(1)} custom-call(s32[1,8]{1,0:T(1,128)S(1)} %bitcast.21, f32[32,1408]{1,0:T(8,128)S(1)} %get-tuple-element.11.rank_rows, f32[32,352]{1,0:T(8,128)S(1)} %get-tuple-element.12.own_rows, bf16[1408,352]{1,0:T(8,128)(2,1)S(1)} %get-tuple-element.13.clear, ...), custom_call_target="tpu_custom_call" | custom-call | flops 2000000000 | bytes 10000000 | tf_op jit(solution)/shard_map/other_flops/pallas_call | solution.py:259
  23.3 0.0 collective-permute-done.2.refs_3_
  23.3 0.3 collective-permute-done.1.refs_2_
  23.6 0.0 collective-permute-done.refs_1_
  23.6 0.0 copy-done.2
  23.6 1.5 %best_response.1 = f32[8,384]{1,0:T(8,128)S(1)} custom-call(s32[1,8]{1,0:T(1,128)S(1)} %bitcast.22, s32[1,8]{1,0:T(1,128)S(1)} %bitcast.23, bf16[8,1408,352]{2,1,0:T(8,128)(2,1)S(1)} %other_flops.1.sums_ref, bf16[1408,352]{1,0:T(8,128)(2,1)S(1)} %get-tuple-element.16.near_ref, f32[32,352]{1,0:T(8,128)S(1)} %action_sums.1.grouped_ref.refs_0_, ...), custom_call_target="tpu_custom_call" | custom-call | flops 1000000000 | bytes 10000000 | tf_op jit(solution)/shard_map/best_response/pallas_call | solution.py:355
  25.2 7.1 %all_to_all.22 = f32[8,1,384]{2,1,0:T(1,128)S(1)} all-to-all(f32[8,1,384]{2,1,0:T(1,128)S(1)} %copy.11), channel_id=1, replica_groups=mesh['board'=8,'hand'=4] {'board'}, dimensions={0} | all-to-all | bytes 24576 | tf_op jit(solution)/shard_map/all_to_all | solution.py:412
  32.3 0.7 %finish.1 = f32[352]{0:T(512)} custom-call(f32[8,384]{1,0:T(8,128)S(1)} %bitcast.18), custom_call_target="tpu_custom_call" | custom-call | bytes 1000000 | tf_op jit(solution)/shard_map/finish/pallas_call | solution.py:374
  (3 shorter events, 0.0 us)
Async XLA Ops:
  0.0 0.7 %copy-start.5 = (f32[44]{0:T(128)S(1)}, f32[44]{0:T(128)}, u32[]{:S(2)}) copy-start(f32[44]{0:T(128)} %param.9) | copy-start | bytes 532
  0.7 8.0 %copy-start.1 = (s32[8]{0:T(128)S(1)}, s32[8]{0:T(128)}, u32[]{:S(2)}) copy-start(s32[8]{0:T(128)} %param.13) | copy-start | bytes 100
  0.7 8.0 %copy-start.3 = (s32[8,8,1408]{2,1,0:T(8,128)S(1)}, s32[8,8,1408]{2,1,0:T(8,128)}, u32[]{:S(2)}) copy-start(s32[8,8,1408]{2,1,0:T(8,128)} %param.11) | copy-start | bytes 1081348
  0.7 8.0 %copy-start.4 = (s32[8,8,5]{1,0,2:T(8,128)S(1)}, s32[8,8,5]{1,0,2:T(8,128)}, u32[]{:S(2)}) copy-start(s32[8,8,5]{1,0,2:T(8,128)} %param.12) | copy-start | bytes 3844
  0.7 8.0 %copy-start.6 = (f32[128]{0:T(128)S(1)}, f32[128]{0:T(128)}, u32[]{:S(2)}) copy-start(f32[128]{0:T(128)} %param.15) | copy-start | bytes 1540
  0.7 8.0 %copy-start.7 = (s32[128]{0:T(128)S(1)}, s32[128]{0:T(128)}, u32[]{:S(2)}) copy-start(s32[128]{0:T(128)} %param.16) | copy-start | bytes 1540
  0.7 8.0 %copy-start.8 = (s32[2,1408]{1,0:T(2,128)S(1)}, s32[2,1408]{1,0:T(2,128)}, u32[]{:S(2)}) copy-start(s32[2,1408]{1,0:T(2,128)} %constant.2.clone.cards_ref) | copy-start | bytes 33796
  0.7 15.1 %copy-start = (bf16[8,128,352]{1,2,0:T(8,128)(2,1)S(1)}, bf16[8,128,352]{1,2,0:T(8,128)(2,1)}, u32[]{:S(2)}) copy-start(bf16[8,128,352]{1,2,0:T(8,128)(2,1)} %param.10) | copy-start | bytes 2162692
  1.3 14.5 %all-to-all-start = ((f32[32,1,44]{2,1,0:T(1,128)}), f32[32,1,44]{2,1,0:T(1,128)S(1)}, u32[]{:S(2)}, u32[]{:S(2)}) async-start(f32[32,1,44]{2,1,0:T(1,128)} %bitcast.8), calls=%async_computation | async-start | bytes 32768 | tf_op jit(solution)/shard_map/all_to_all | solution.py:391
  16.4 7.0 %collective-permute-start.2 = (f32[32,352]{1,0:T(8,128)S(1)}, f32[32,352]{1,0:T(8,128)S(1)}, u32[]{:S(2)}, u32[]{:S(2)}) collective-permute-start(f32[32,352]{1,0:T(8,128)S(1)} %action_sums.1.grouped_ref.refs_0_), channel_id=1, source_target_pairs={{0,3},{1,2},{2,1},{3,0},{4,7},{5,6},{6,5},{7,4},{8,11},{9,10},{10,... | collective-permute-start | bytes 135176 | tf_op jit(solution)/shard_map/ppermute | solution.py:407
  17.0 6.6 %collective-permute-start.1 = (f32[32,352]{1,0:T(8,128)S(1)}, f32[32,352]{1,0:T(8,128)S(1)}, u32[]{:S(2)}, u32[]{:S(2)}) collective-permute-start(f32[32,352]{1,0:T(8,128)S(1)} %action_sums.1.grouped_ref.refs_0_), channel_id=1, source_target_pairs={{0,2},{1,3},{2,0},{3,1},{4,6},{5,7},{6,4},{7,5},{8,10},{9,11},{10,... | collective-permute-start | bytes 135176 | tf_op jit(solution)/shard_map/ppermute | solution.py:407
  18.4 5.2 %collective-permute-start = (f32[32,352]{1,0:T(8,128)S(1)}, f32[32,352]{1,0:T(8,128)S(1)}, u32[]{:S(2)}, u32[]{:S(2)}) collective-permute-start(f32[32,352]{1,0:T(8,128)S(1)} %action_sums.1.grouped_ref.refs_0_), channel_id=1, source_target_pairs={{0,1},{1,0},{2,3},{3,2},{4,5},{5,4},{6,7},{7,6},{8,9},{9,8},{10,11... | collective-permute-start | bytes 135176 | tf_op jit(solution)/shard_map/ppermute | solution.py:407
  20.8 2.8 %copy-start.2 = (s32[8]{0:T(128)S(1)}, s32[8]{0:T(128)}, u32[]{:S(2)}) copy-start(s32[8]{0:T(128)} %param.14) | copy-start | bytes 100

commit v3 on v2

--- a/solution.py
+++ b/solution.py
@@ -13,12 +13,12 @@
 ACTS = 3
 CARDS = 64
 DEAD_CARD = 52
-GROUP = 4
 SPLITS = 3
 PART = 4
 FAR = 40
 FAR_FLOPS = 24
 RANKS = 128
+FEW = 8
 USED_RANKS = 96
 NO_RANK = 127.0
 
@@ -64,61 +64,84 @@
     return lax.broadcasted_iota(jnp.int32, (USED_RANKS, width), 0).astype(jnp.float32)
 
 
-def add_flops(first, last, counts, rank_rows, own_rows, clear, holds, signs, sums_ref, sent):
+def slot_parts(slots):
+    return [slice(low, min(low + 256, slots)) for low in range(0, slots, 256)]
+
+
+def add_flops(first, last, rows_from, counts, rank_rows, own_rows, clear, holds, signs, place, sent):
     slots, rows = clear.shape
     runouts = holds.shape[0] // RANKS
     for low in range(0, runouts * RANKS, RANKS):
         holds[low + USED_RANKS : low + RANKS, :] = jnp.zeros((RANKS - USED_RANKS, slots), EXACT)
         signs[low + USED_RANKS : low + RANKS, :] = jnp.zeros((RANKS - USED_RANKS, rows), EXACT)
 
-    one, zero = jnp.ones((32, slots), EXACT), jnp.zeros((32, slots), EXACT)
-    down = lax.broadcasted_iota(jnp.int32, one.shape, 0)
-
-    def add_runout(at, low):
-        span = pl.ds(pl.multiple_of(low, RANKS), USED_RANKS)
-        rank = jnp.broadcast_to(rank_rows[pl.ds(at, 1), :].astype(jnp.int32), one.shape)
+    parts = slot_parts(slots)
+    tile = 32
+
+    def hold(rank, low, part):
+        shape = (tile, part.stop - part.start)
+        rank = jnp.broadcast_to(rank[:, part].astype(jnp.int32), shape)
         rank = rank.astype(jnp.int8)
-        for step in range(0, USED_RANKS, one.shape[0]):
+        down = lax.broadcasted_iota(jnp.int32, shape, 0)
+        one, zero = jnp.ones(shape, EXACT), jnp.zeros(shape, EXACT)
+        for step in range(0, USED_RANKS, tile):
             held = jnp.where(rank == (down + step).astype(jnp.int8), one, zero)
-            holds[pl.ds(pl.multiple_of(low + step, one.shape[0]), one.shape[0]), :] = held
+            holds[pl.ds(low + step, tile), part] = held
+
+    def sign(at, low):
         rank = own_rows[pl.ds(at, 1), :]
         live = jnp.where(rank < NO_RANK, 1.0, 0.0)
-        sign = jnp.minimum(jnp.maximum(rank - level(rows), -1.0), 1.0)
-        signs[span, :] = (sign * live).astype(EXACT)
-
-    def multiply(flop, depth):
-        right = signs[:depth, :]
-        for lane in range(0, slots, 256):
-            part = slice(lane, min(lane + 256, slots))
-            sign = lax.dot_general(holds[:depth, part], right, TN, preferred_element_type=jnp.float32)
-            sums_ref[flop, part, :] = sign.astype(jnp.bfloat16) * clear[part, :]
+        against = jnp.minimum(jnp.maximum(rank - level(rows), -1.0), 1.0)
+        signs[pl.ds(low, USED_RANKS), :] = (against * live).astype(EXACT)
+
+    def multiply(flop, depth, part):
+        product = lax.dot_general(
+            holds[:depth, part], signs[:depth, :], TN, preferred_element_type=jnp.float32
+        )
+        target, index = place(flop, part)
+        target[index] = product.astype(jnp.bfloat16) * clear[part, :]
 
     def one_flop(flop, carry):
         count = counts[flop]
-
-        def one_runout(runout, carry):
-            add_runout((flop - first) * runouts + runout, runout * RANKS)
-            return carry
-
-        lax.fori_loop(0, count, one_runout, 0)
-
-        @pl.when((lax.rem(count, 2) == 1) & (count > 1))
+        row = (flop - rows_from) * runouts
+
+        for few in range(1, FEW + 1):
+
+            @pl.when(count == few)
+            def _():
+                for runout in range(few):
+                    sign(row + runout, runout * RANKS)
+                ranks = [rank_rows[pl.ds(row + runout, 1), :] for runout in range(few)]
+                for chunk, part in enumerate(parts):
+                    for runout, rank in enumerate(ranks):
+                        hold(rank, runout * RANKS, part)
+                    multiply(flop, few * RANKS, part)
+                    sent(flop, chunk, part)
+
+        @pl.when(count > FEW)
         def _():
-            span = pl.ds(pl.multiple_of(count * RANKS, RANKS), RANKS)
-            holds[span, :] = jnp.zeros((RANKS, slots), EXACT)
-            signs[span, :] = jnp.zeros((RANKS, rows), EXACT)
-
-        @pl.when(count == 1)
-        def _():
-            multiply(flop, RANKS)
-
-        for step in range(2, runouts + 1, 2):
-
-            @pl.when((count == step) | ((count == step - 1) & (count > 1)))
+            def one_runout(runout, carry):
+                low = pl.multiple_of(runout * RANKS, RANKS)
+                hold(rank_rows[pl.ds(row + runout, 1), :], low, slice(0, slots))
+                sign(row + runout, low)
+                return carry
+
+            lax.fori_loop(0, count, one_runout, 0)
+
+            @pl.when(lax.rem(count, 2) == 1)
             def _():
-                multiply(flop, step * RANKS)
-
-        sent(flop)
+                span = pl.ds(pl.multiple_of(count * RANKS, RANKS), RANKS)
+                holds[span, :] = jnp.zeros((RANKS, slots), EXACT)
+                signs[span, :] = jnp.zeros((RANKS, rows), EXACT)
+
+        for step in range(FEW + 2, runouts + 1, 2):
+
+            @pl.when((count == step) | (count == step - 1))
+            def _():
+                for chunk, part in enumerate(parts):
+                    multiply(flop, step * RANKS, part)
+                    sent(flop, chunk, part)
+
         return carry
 
     lax.fori_loop(first, last, one_flop, 0)
@@ -179,20 +202,25 @@
     weights = jnp.where(row == act, jnp.broadcast_to(pot_ref[...], row.shape), 0.0)
     weights_ref[...] = jnp.concatenate(split_bf16(weights), axis=0).astype(jnp.bfloat16)
 
-    def copy(flop):
-        return pltpu.make_async_copy(sums.at[flop], far_ref.at[flop], sem.at[flop])
-
-    def sent(flop):
-        @pl.when(flop < last)
-        def _():
-            copy(flop).start()
-
-    last = sums.shape[0] - 1
+    def copy(flop, chunk, part):
+        span = pl.ds(part.start, part.stop - part.start)
+        return pltpu.make_async_copy(
+            sums.at[flop, span], far_ref.at[flop, span], sem.at[flop, chunk]
+        )
+
+    last = sums.shape[0]
     tables = (counts, rank_rows, own_rows, clear, holds, signs)
-    add_flops(0, last + 1, *tables, sums, sent)
-    near_ref[...] = sums[last]
+    add_flops(
+        0, last, 0, *tables,
+        lambda flop, part: (sums, (flop, part)),
+        lambda flop, chunk, part: copy(flop, chunk, part).start(),
+    )
+    add_flops(
+        last, last + 1, 0, *tables, lambda flop, part: (near_ref, part), lambda *done: None
+    )
     for flop in range(last):
-        copy(flop).wait()
+        for chunk, part in enumerate(slot_parts(slots)):
+            copy(flop, chunk, part).wait()
 
 
 def read_counts(count_ref, counts):
@@ -228,8 +256,8 @@
         + [
             pltpu.VMEM((total, slots), jnp.float32),
             pltpu.VMEM((total, rows), jnp.float32),
-            pltpu.VMEM((part, slots, rows), jnp.bfloat16),
-            pltpu.SemaphoreType.DMA((part - 1,)),
+            pltpu.VMEM((part - 1, slots, rows), jnp.bfloat16),
+            pltpu.SemaphoreType.DMA((part - 1, len(slot_parts(slots)))),
         ],
         name="first_flops",
         **params(FAR, 2 * 10**9, 10**7),
@@ -248,7 +276,11 @@
     for copy in copies:
         copy.start()
     tables = (counts, rank_rows, own_rows, clear, holds, signs)
-    add_flops(part, count_ref.shape[1], *tables, sums_ref, lambda flop: None)
+    add_flops(
+        part, count_ref.shape[1], part, *tables,
+        lambda flop, part: (sums_ref, (flop, part)),
+        lambda *done: None,
+    )
     for copy in copies:
         copy.wait()
 
@@ -304,14 +336,14 @@
         line_reach = (strategy_ref[flop].astype(jnp.float32) * scale).astype(jnp.bfloat16)
         parts = lax.dot_general(weights, line_reach, NT, preferred_element_type=jnp.float32)
         sums = parts[0:8] + parts[8:16] + parts[16:24]
-        out_ref[flop * GROUP : (flop + 1) * GROUP, :] = sums[0:GROUP]
+        out_ref[flop * ACTS : (flop + 1) * ACTS, :] = sums[0:ACTS]
 
 
 def action_sums(reach, strategy, weights):
     flops, rows, lines = strategy.shape
     return pl.pallas_call(
         action_kernel,
-        out_shape=jax.ShapeDtypeStruct((flops * GROUP, rows), jnp.float32),
+        out_shape=jax.ShapeDtypeStruct((flops * ACTS, rows), jnp.float32),
         in_specs=[VMEM] * 3,
         out_specs=VMEM,
         name="action_sums",
@@ -319,20 +351,25 @@
     )(reach, strategy, weights)
 
 
+def row_span(flop):
+    low = flop * ACTS // 8 * 8
+    return low, (flop * ACTS + ACTS + 7) // 8 * 8
+
+
 def response_kernel(single, count_ref, weight_ref, sums_ref, near_ref, *refs):
     shards, out_ref, products = refs[:-2], refs[-2], refs[-1]
     flops, slots, rows = sums_ref.shape
-    gathered = jnp.zeros((flops * GROUP, slots), jnp.float32)
+    gathered = jnp.zeros((flops * ACTS, slots), jnp.float32)
     for step, shard in enumerate(shards):
         at = jnp.bitwise_xor(lax.axis_index("hand"), step) * rows
-        empty = jnp.zeros((flops * GROUP, slots - rows), jnp.float32)
+        empty = jnp.zeros((flops * ACTS, slots - rows), jnp.float32)
         gathered = gathered + pltpu.roll(jnp.concatenate([shard[...], empty], axis=1), at, 1)
     splits = split_bf16(gathered)
     for flop in range(flops):
         matrix = near_ref if flop == single else sums_ref.at[flop]
-        low = flop * GROUP // 8 * 8
-        left = jnp.concatenate([part[low : low + 8] for part in splits], axis=0)
-        products[flop] = jnp.dot(
+        low, high = row_span(flop)
+        left = jnp.concatenate([part[low:high] for part in splits], axis=0)
+        products[flop, : left.shape[0]] = jnp.dot(
             left.astype(jnp.bfloat16), matrix[...], preferred_element_type=jnp.float32
         )
 
@@ -340,8 +377,9 @@
     weights = weight_ref[...].astype(jnp.float32)
     counts = count_ref[...].astype(jnp.float32)
     for flop in range(flops):
-        group = products[flop, 0:8] + products[flop, 8:16] + products[flop, 16:24]
-        at = flop * GROUP % 8
+        low, high = row_span(flop)
+        size, at = high - low, flop * ACTS - low
+        group = sum(products[flop, part * size : (part + 1) * size] for part in range(SPLITS))
         best = jnp.max(group[at : at + ACTS], axis=0, keepdims=True)
         values = values + best * weights[:, flop : flop + 1] / counts[:, flop : flop + 1]
     tail = jnp.sum(weights, axis=1, keepdims=True)
@@ -357,7 +395,7 @@
         out_shape=jax.ShapeDtypeStruct((copies, width), jnp.float32),
         in_specs=[VMEM] * (4 + len(shards)),
         out_specs=VMEM,
-        scratch_shapes=[pltpu.VMEM((sums.shape[0], 8 * SPLITS, rows), jnp.float32)],
+        scratch_shapes=[pltpu.VMEM((sums.shape[0], 16 * SPLITS, rows), jnp.float32)],
         name="best_response",
         **params(12, 10**9, 10**7),
     )(counts, weights, sums, near, *shards)

time: 33.2 us -> 32.6 us (0.982)
  Pallas kernels: 9.9 us -> 8.73 us
  waiting for transfers between devices: 3.33 us -> 3.79 us
    all_to_all x1, waiting for transfers between devices: 3.05 us -> 3.78 us  [body(): reach = lax.all_to_all(send, ('board', 'hand'), 0, 0, tiled=True)]
    pallas_call x1, Pallas kernels: 4.05 us -> 3.32 us  [first_flops(): pl.pallas_call(first_kernel, out_shape=[jax.ShapeDtypeStruct((FAR_FLOPS,...]
    pallas_call x1, Pallas kernels: 2.49 us -> 2.07 us  [other_flops(): pl.pallas_call(functools.partial(other_kernel, part), out_shape=jax.Shape...]
  transfers between devices with their start and end apart: 4 -> 4, of which waited for: 2 -> 1; matrix products, arithmetic and copies ran while one was open for 0% -> 0% of each run, Pallas kernels for 20% -> 17%
where the time goes in v3:
time: 32.6 us; the launch traced here: 32.2 us
  starting transfers between devices  11.8 us (36%)
  Pallas kernels  8.73 us (27%)
  blocking collectives  7.1 us (22%)
  waiting for transfers between devices  3.79 us (12%)
  local copies, waits for them, and re-layouts  0.7 us (2%)
    all_to_all x1, starting transfers between devices, body(): reach = lax.all_to_all(send, ('board', 'hand'), 0, 0, tiled=True)  7.3 us
    all_to_all x1, blocking collectives, body(): return finish(lax.all_to_all(partial, 'board', 0, 0, tiled=True), rows)  7.1 us
    ppermute x3, starting transfers between devices, body(): shards.append(lax.ppermute(grouped, 'hand', swap))  4.45 us
    all_to_all x1, waiting for transfers between devices, body(): reach = lax.all_to_all(send, ('board', 'hand'), 0, 0, tiled=True)  3.78 us
    pallas_call x1, Pallas kernels, first_flops(): pl.pallas_call(first_kernel, out_shape=[jax.ShapeDtypeStruct((FAR_FLOPS,...  3.32 us
    pallas_call x1, Pallas kernels, other_flops(): pl.pallas_call(functools.partial(other_kernel, part), out_shape=jax.Shape...  2.07 us
    pallas_call x1, Pallas kernels, best_response(): pl.pallas_call(functools.partial(response_kernel, single), out_shape=jax....  1.5 us
    unnamed x19, local copies, waits for them, and re-layouts  0.69 us
  transfers between devices with their start and end apart: 4, of which 1 were waited for; matrix products, arithmetic and copies ran while one was open for 0% of the time, Pallas kernels for 17%

profile of v3, /device:TPU:0, one launch (start us, length us, event | category | flops | bytes accessed | tf_op | source)
XLA Modules:
  0.0 32.2 jit_solution(11917739420219774792)
XLA Ops:
  0.0 0.0 copy-start.5
  0.0 0.7 %copy-done.5 = f32[44]{0:T(128)S(1)} copy-done((f32[44]{0:T(128)S(1)}, f32[44]{0:T(128)}, u32[]{:S(2)}) %copy-start.5) | copy-done | bytes 200
  0.7 0.0 copy-start.1
  0.7 0.0 copy-start.3
  0.7 0.0 copy-start.4
  0.7 0.0 copy-start.6
  0.7 0.0 copy-start.7
  0.7 0.0 copy-start.8
  0.7 0.0 copy-start
  0.7 0.6 %reach_copies.1 = f32[32,44]{1,0:T(8,128)} custom-call(f32[1,44]{1,0:T(1,128)S(1)} %bitcast.26), custom_call_target="tpu_custom_call" | custom-call | flops 10000000000 | bytes 100000000 | tf_op jit(solution)/shard_map/reach_copies/pallas_call | solution.py:53
  1.3 7.3 %all-to-all-start = ((f32[32,1,44]{2,1,0:T(1,128)}), f32[32,1,44]{2,1,0:T(1,128)S(1)}, u32[]{:S(2)}, u32[]{:S(2)}) async-start(f32[32,1,44]{2,1,0:T(1,128)} %bitcast.8), calls=%async_computation | async-start | bytes 32768 | tf_op jit(solution)/shard_map/all_to_all | solution.py:429
  8.6 0.0 copy-done.1
  8.6 0.0 copy-done.3
  8.6 0.0 copy-done.4
  8.6 0.0 copy-done.6
  8.6 0.0 copy-done.7
  8.7 0.0 copy-done.8
  8.7 3.3 %first_flops.1 = (bf16[24,1408,352]{2,1,0:T(8,128)(2,1)}, bf16[1408,352]{1,0:T(8,128)(2,1)S(1)}, f32[32,1408]{1,0:T(8,128)S(1)}, f32[32,352]{1,0:T(8,128)S(1)}, ...) custom-call(s32[1,8]{1,0:T(1,128)S(1)} %bitcast.20, s32[64,1408]{1,0:T(8,128)S(1)} %bitcast.24, ...), custom_call_target="tpu_custom_call" | custom-call | flops 2000000000 | bytes 10000000 | tf_op jit(solution)/shard_map/first_flops/pallas_call | solution.py:243
  12.0 3.8 %all-to-all-done = f32[32,1,44]{2,1,0:T(1,128)S(1)} async-done(((f32[32,1,44]{2,1,0:T(1,128)}), f32[32,1,44]{2,1,0:T(1,128)S(1)}, u32[]{:S(2)}, u32[]{:S(2)}) %all-to-all-start) | async-done | bytes 5664 | tf_op jit(solution)/shard_map/all_to_all | solution.py:429
  15.8 0.0 copy-done
  15.8 0.6 %action_sums.1.grouped_ref.refs_0_ = f32[24,352]{1,0:T(8,128)S(1)} custom-call(f32[32,44]{1,0:T(8,128)S(1)} %bitcast.17, bf16[8,352,128]{2,1,0:T(8,128)(2,1)S(1)} %bitcast.16, bf16[24,128]{1,0:T(8,128)(2,1)S(1)} %get-tuple-element.14.weights_ref), custom_call_target="tpu_custom_call" | custom-call | flops 100000000 | bytes 1000000 | tf_op jit(solution)/shard_map/action_sums/pallas_call | solution.py:344
  16.4 0.6 %collective-permute-start.2 = (f32[24,352]{1,0:T(8,128)S(1)}, f32[24,352]{1,0:T(8,128)S(1)}, u32[]{:S(2)}, u32[]{:S(2)}) collective-permute-start(f32[24,352]{1,0:T(8,128)S(1)} %action_sums.1.grouped_ref.refs_0_), channel_id=1, source_target_pairs={{0,3},{1,2},{2,1},{3,0},{4,7},{5,6},{6,5},{7,4},{8,11},{9,10},{10,... | collective-permute-start | bytes 101384 | tf_op jit(solution)/shard_map/ppermute | solution.py:445
  16.9 1.4 %collective-permute-start.1 = (f32[24,352]{1,0:T(8,128)S(1)}, f32[24,352]{1,0:T(8,128)S(1)}, u32[]{:S(2)}, u32[]{:S(2)}) collective-permute-start(f32[24,352]{1,0:T(8,128)S(1)} %action_sums.1.grouped_ref.refs_0_), channel_id=1, source_target_pairs={{0,2},{1,3},{2,0},{3,1},{4,6},{5,7},{6,4},{7,5},{8,10},{9,11},{10,... | collective-permute-start | bytes 101384 | tf_op jit(solution)/shard_map/ppermute | solution.py:445
  18.4 2.4 %collective-permute-start = (f32[24,352]{1,0:T(8,128)S(1)}, f32[24,352]{1,0:T(8,128)S(1)}, u32[]{:S(2)}, u32[]{:S(2)}) collective-permute-start(f32[24,352]{1,0:T(8,128)S(1)} %action_sums.1.grouped_ref.refs_0_), channel_id=1, source_target_pairs={{0,1},{1,0},{2,3},{3,2},{4,5},{5,4},{6,7},{7,6},{8,9},{9,8},{10,11... | collective-permute-start | bytes 101384 | tf_op jit(solution)/shard_map/ppermute | solution.py:445
  20.8 2.1 %other_flops.1.sums_ref = bf16[8,1408,352]{2,1,0:T(8,128)(2,1)S(1)} custom-call(s32[1,8]{1,0:T(1,128)S(1)} %bitcast.21, f32[32,1408]{1,0:T(8,128)S(1)} %get-tuple-element.11.rank_rows, f32[32,352]{1,0:T(8,128)S(1)} %get-tuple-element.12.own_rows, bf16[1408,352]{1,0:T(8,128)(2,1)S(1)} %get-tuple-element.13.clear, ...), custom_call_target="tpu_custom_call" | custom-call | flops 2000000000 | bytes 10000000 | tf_op jit(solution)/shard_map/other_flops/pallas_call | solution.py:291
  22.9 0.0 collective-permute-done.2.refs_3_
  22.9 0.0 collective-permute-done.1.refs_2_
  22.9 0.0 collective-permute-done.refs_1_
  22.9 0.0 copy-done.2
  23.0 1.5 %best_response.1 = f32[8,384]{1,0:T(8,128)S(1)} custom-call(s32[1,8]{1,0:T(1,128)S(1)} %bitcast.22, s32[1,8]{1,0:T(1,128)S(1)} %bitcast.23, bf16[8,1408,352]{2,1,0:T(8,128)(2,1)S(1)} %other_flops.1.sums_ref, bf16[1408,352]{1,0:T(8,128)(2,1)S(1)} %get-tuple-element.16.near_ref, f32[24,352]{1,0:T(8,128)S(1)} %action_sums.1.grouped_ref.refs_0_, ...), custom_call_target="tpu_custom_call" | custom-call | flops 1000000000 | bytes 10000000 | tf_op jit(solution)/shard_map/best_response/pallas_call | solution.py:393
  24.5 7.1 %all_to_all.22 = f32[8,1,384]{2,1,0:T(1,128)S(1)} all-to-all(f32[8,1,384]{2,1,0:T(1,128)S(1)} %copy.11), channel_id=1, replica_groups=mesh['board'=8,'hand'=4] {'board'}, dimensions={0} | all-to-all | bytes 24576 | tf_op jit(solution)/shard_map/all_to_all | solution.py:450
  31.6 0.7 %finish.1 = f32[352]{0:T(512)} custom-call(f32[8,384]{1,0:T(8,128)S(1)} %bitcast.18), custom_call_target="tpu_custom_call" | custom-call | bytes 1000000 | tf_op jit(solution)/shard_map/finish/pallas_call | solution.py:412
  (3 shorter events, 0.0 us)
Async XLA Ops:
  0.0 0.7 %copy-start.5 = (f32[44]{0:T(128)S(1)}, f32[44]{0:T(128)}, u32[]{:S(2)}) copy-start(f32[44]{0:T(128)} %param.9) | copy-start | bytes 532
  0.7 8.0 %copy-start.1 = (s32[8]{0:T(128)S(1)}, s32[8]{0:T(128)}, u32[]{:S(2)}) copy-start(s32[8]{0:T(128)} %param.13) | copy-start | bytes 100
  0.7 8.0 %copy-start.3 = (s32[8,8,1408]{2,1,0:T(8,128)S(1)}, s32[8,8,1408]{2,1,0:T(8,128)}, u32[]{:S(2)}) copy-start(s32[8,8,1408]{2,1,0:T(8,128)} %param.11) | copy-start | bytes 1081348
  0.7 8.0 %copy-start.4 = (s32[8,8,5]{1,0,2:T(8,128)S(1)}, s32[8,8,5]{1,0,2:T(8,128)}, u32[]{:S(2)}) copy-start(s32[8,8,5]{1,0,2:T(8,128)} %param.12) | copy-start | bytes 3844
  0.7 8.0 %copy-start.6 = (f32[128]{0:T(128)S(1)}, f32[128]{0:T(128)}, u32[]{:S(2)}) copy-start(f32[128]{0:T(128)} %param.15) | copy-start | bytes 1540
  0.7 8.0 %copy-start.7 = (s32[128]{0:T(128)S(1)}, s32[128]{0:T(128)}, u32[]{:S(2)}) copy-start(s32[128]{0:T(128)} %param.16) | copy-start | bytes 1540
  0.7 8.0 %copy-start.8 = (s32[2,1408]{1,0:T(2,128)S(1)}, s32[2,1408]{1,0:T(2,128)}, u32[]{:S(2)}) copy-start(s32[2,1408]{1,0:T(2,128)} %constant.2.clone.cards_ref) | copy-start | bytes 33796
  0.7 15.1 %copy-start = (bf16[8,128,352]{1,2,0:T(8,128)(2,1)S(1)}, bf16[8,128,352]{1,2,0:T(8,128)(2,1)}, u32[]{:S(2)}) copy-start(bf16[8,128,352]{1,2,0:T(8,128)(2,1)} %param.10) | copy-start | bytes 2162692
  1.3 14.5 %all-to-all-start = ((f32[32,1,44]{2,1,0:T(1,128)}), f32[32,1,44]{2,1,0:T(1,128)S(1)}, u32[]{:S(2)}, u32[]{:S(2)}) async-start(f32[32,1,44]{2,1,0:T(1,128)} %bitcast.8), calls=%async_computation | async-start | bytes 32768 | tf_op jit(solution)/shard_map/all_to_all | solution.py:429
  16.4 6.5 %collective-permute-start.2 = (f32[24,352]{1,0:T(8,128)S(1)}, f32[24,352]{1,0:T(8,128)S(1)}, u32[]{:S(2)}, u32[]{:S(2)}) collective-permute-start(f32[24,352]{1,0:T(8,128)S(1)} %action_sums.1.grouped_ref.refs_0_), channel_id=1, source_target_pairs={{0,3},{1,2},{2,1},{3,0},{4,7},{5,6},{6,5},{7,4},{8,11},{9,10},{10,... | collective-permute-start | bytes 101384 | tf_op jit(solution)/shard_map/ppermute | solution.py:445
  16.9 6.0 %collective-permute-start.1 = (f32[24,352]{1,0:T(8,128)S(1)}, f32[24,352]{1,0:T(8,128)S(1)}, u32[]{:S(2)}, u32[]{:S(2)}) collective-permute-start(f32[24,352]{1,0:T(8,128)S(1)} %action_sums.1.grouped_ref.refs_0_), channel_id=1, source_target_pairs={{0,2},{1,3},{2,0},{3,1},{4,6},{5,7},{6,4},{7,5},{8,10},{9,11},{10,... | collective-permute-start | bytes 101384 | tf_op jit(solution)/shard_map/ppermute | solution.py:445
  18.4 4.5 %collective-permute-start = (f32[24,352]{1,0:T(8,128)S(1)}, f32[24,352]{1,0:T(8,128)S(1)}, u32[]{:S(2)}, u32[]{:S(2)}) collective-permute-start(f32[24,352]{1,0:T(8,128)S(1)} %action_sums.1.grouped_ref.refs_0_), channel_id=1, source_target_pairs={{0,1},{1,0},{2,3},{3,2},{4,5},{5,4},{6,7},{7,6},{8,9},{9,8},{10,11... | collective-permute-start | bytes 101384 | tf_op jit(solution)/shard_map/ppermute | solution.py:445
  20.8 2.1 %copy-start.2 = (s32[8]{0:T(128)S(1)}, s32[8]{0:T(128)}, u32[]{:S(2)}) copy-start(s32[8]{0:T(128)} %param.14) | copy-start | bytes 100

commit v4 on v3

--- a/solution.py
+++ b/solution.py
@@ -18,7 +18,6 @@
 FAR = 40
 FAR_FLOPS = 24
 RANKS = 128
-FEW = 8
 USED_RANKS = 96
 NO_RANK = 127.0
 
@@ -105,7 +104,7 @@
         count = counts[flop]
         row = (flop - rows_from) * runouts
 
-        for few in range(1, FEW + 1):
+        for few in range(1, runouts + 1):
 
             @pl.when(count == few)
             def _():
@@ -116,30 +115,6 @@
                     for runout, rank in enumerate(ranks):
                         hold(rank, runout * RANKS, part)
                     multiply(flop, few * RANKS, part)
-                    sent(flop, chunk, part)
-
-        @pl.when(count > FEW)
-        def _():
-            def one_runout(runout, carry):
-                low = pl.multiple_of(runout * RANKS, RANKS)
-                hold(rank_rows[pl.ds(row + runout, 1), :], low, slice(0, slots))
-                sign(row + runout, low)
-                return carry
-
-            lax.fori_loop(0, count, one_runout, 0)
-
-            @pl.when(lax.rem(count, 2) == 1)
-            def _():
-                span = pl.ds(pl.multiple_of(count * RANKS, RANKS), RANKS)
-                holds[span, :] = jnp.zeros((RANKS, slots), EXACT)
-                signs[span, :] = jnp.zeros((RANKS, rows), EXACT)
-
-        for step in range(FEW + 2, runouts + 1, 2):
-
-            @pl.when((count == step) | (count == step - 1))
-            def _():
-                for chunk, part in enumerate(parts):
-                    multiply(flop, step * RANKS, part)
                     sent(flop, chunk, part)
 
         return carry
@@ -401,9 +376,10 @@
     )(counts, weights, sums, near, *shards)
 
 
-def finish_kernel(parts_ref, out_ref):
+def finish_kernel(*refs):
+    parts, out_ref = refs[:-1], refs[-1]
     rows = out_ref.shape[0]
-    whole = jnp.sum(parts_ref[...], axis=0)
+    whole = sum(part[0] for part in parts)
     weight = whole[rows : rows + 1]
     out_ref[...] = whole[:rows] / weight
 
@@ -412,11 +388,25 @@
     return pl.pallas_call(
         finish_kernel,
         out_shape=jax.ShapeDtypeStruct((rows,), jnp.float32),
-        in_specs=[VMEM],
+        in_specs=[VMEM] * len(parts),
         out_specs=VMEM,
         name="finish",
         **params(2),
-    )(parts)
+    )(*parts)
+
+
+def board_parts(partial, boards_n):
+    def swapped(values, mask):
+        return lax.ppermute(values, "board", [(at, at ^ mask) for at in range(boards_n)])
+
+    values, bit = partial + swapped(partial, 1), 2
+    while True:
+        masks = [bit, 2 * bit, 3 * bit] if 2 * bit < boards_n else [bit]
+        parts = [values] + [swapped(values, mask) for mask in masks]
+        bit *= 4
+        if bit >= boards_n:
+            return parts
+        values = sum(parts)
 
 
 def body(boards_n, hands_n, reach_pre, strategy, ranks, boards, river_live, iso_weight, pot, line_act):
@@ -446,8 +436,8 @@
     sums = other_flops(part, counts, *tables, grouped, far)
 
     weights = iso_weight.reshape(1, flops)
-    partial = best_response(part - 1, counts, weights, sums, near, shards, boards_n)
-    return finish(lax.all_to_all(partial, "board", 0, 0, tiled=True), rows)
+    partial = best_response(part - 1, counts, weights, sums, near, shards, 1)
+    return finish(board_parts(partial, boards_n), rows)
 
 
 def solution(mesh):

time: 32.6 us -> 32.4 us (level)
  blocking collectives: 7.1 us -> 0 us
  starting transfers between devices: 11.8 us -> 15.3 us
  waiting for transfers between devices: 3.79 us -> 6.04 us
  Pallas kernels: 8.73 us -> 10 us
    all_to_all x1 -> x0, blocking collectives: 7.1 us -> none  [body(): return finish(lax.all_to_all(partial, 'board', 0, 0, tiled=True), rows)]
    ppermute x0 -> x4, starting transfers between devices: none -> 3.56 us  [swapped(): lax.ppermute(values, 'board', [(at, at ^ mask) for at in range(boards_n)])]
    ppermute x0 -> x4, waiting for transfers between devices: none -> 2.69 us  [swapped(): lax.ppermute(values, 'board', [(at, at ^ mask) for at in range(boards_n)])]
    pallas_call x1, Pallas kernels: 2.07 us -> 2.93 us  [other_flops(): pl.pallas_call(functools.partial(other_kernel, part), out_shape=jax.Shape...]
    all_to_all x1, waiting for transfers between devices: 3.78 us -> 3.34 us  [body(): reach = lax.all_to_all(send, ('board', 'hand'), 0, 0, tiled=True)]
    pallas_call x1, Pallas kernels: 3.32 us -> 3.76 us  [first_flops(): pl.pallas_call(first_kernel, out_shape=[jax.ShapeDtypeStruct((FAR_FLOPS,...]
    unnamed x19 -> x18, local copies, waits for them, and re-layouts: 0.69 us -> 0.69 us
  transfers between devices with their start and end apart: 4 -> 8, of which waited for: 1 -> 4; matrix products, arithmetic and copies ran while one was open for 0% -> 0% of each run, Pallas kernels for 17% -> 21%
where the time goes in v4:
time: 32.4 us; the launch traced here: 32.2 us
  starting transfers between devices  15.3 us (47%)
  Pallas kernels  10 us (31%)
  waiting for transfers between devices  6.04 us (19%)
  local copies, waits for them, and re-layouts  0.69 us (2%)
    all_to_all x1, starting transfers between devices, body(): reach = lax.all_to_all(send, ('board', 'hand'), 0, 0, tiled=True)  7.3 us
    ppermute x3, starting transfers between devices, body(): shards.append(lax.ppermute(grouped, 'hand', swap))  4.45 us
    pallas_call x1, Pallas kernels, first_flops(): pl.pallas_call(first_kernel, out_shape=[jax.ShapeDtypeStruct((FAR_FLOPS,...  3.76 us
    ppermute x4, starting transfers between devices, swapped(): lax.ppermute(values, 'board', [(at, at ^ mask) for at in range(boards_n)])  3.56 us
    all_to_all x1, waiting for transfers between devices, body(): reach = lax.all_to_all(send, ('board', 'hand'), 0, 0, tiled=True)  3.34 us
    pallas_call x1, Pallas kernels, other_flops(): pl.pallas_call(functools.partial(other_kernel, part), out_shape=jax.Shape...  2.93 us
    ppermute x4, waiting for transfers between devices, swapped(): lax.ppermute(values, 'board', [(at, at ^ mask) for at in range(boards_n)])  2.69 us
    pallas_call x1, Pallas kernels, best_response(): pl.pallas_call(functools.partial(response_kernel, single), out_shape=jax....  1.5 us
  transfers between devices with their start and end apart: 8, of which 4 were waited for; matrix products, arithmetic and copies ran while one was open for 0% of the time, Pallas kernels for 21%

profile of v4, /device:TPU:0, one launch (start us, length us, event | category | flops | bytes accessed | tf_op | source)
XLA Modules:
  0.0 32.2 jit_solution(15143789434325773993)
XLA Ops:
  0.0 0.7 %copy-done.5 = f32[44]{0:T(128)S(1)} copy-done((f32[44]{0:T(128)S(1)}, f32[44]{0:T(128)}, u32[]{:S(2)}) %copy-start.5) | copy-done | bytes 200
  0.7 0.0 copy-start.7
  0.7 0.0 copy-start.8
  0.7 0.0 copy-start
  0.7 0.6 %reach_copies.1 = f32[32,44]{1,0:T(8,128)} custom-call(f32[1,44]{1,0:T(1,128)S(1)} %bitcast.20), custom_call_target="tpu_custom_call" | custom-call | flops 10000000000 | bytes 100000000 | tf_op jit(solution)/shard_map/reach_copies/pallas_call | solution.py:52
  1.3 7.3 %all-to-all-start = ((f32[32,1,44]{2,1,0:T(1,128)}), f32[32,1,44]{2,1,0:T(1,128)S(1)}, u32[]{:S(2)}, u32[]{:S(2)}) async-start(f32[32,1,44]{2,1,0:T(1,128)} %bitcast.8), calls=%async_computation | async-start | bytes 32768 | tf_op jit(solution)/shard_map/all_to_all | solution.py:419
  8.6 0.0 copy-done.1
  8.6 0.0 copy-done.3
  8.6 0.0 copy-done.4
  8.6 0.0 copy-done.6
  8.6 0.0 copy-done.7
  8.7 0.0 copy-done.8
  8.7 3.8 %first_flops.1 = (bf16[24,1408,352]{2,1,0:T(8,128)(2,1)}, bf16[1408,352]{1,0:T(8,128)(2,1)S(1)}, f32[32,1408]{1,0:T(8,128)S(1)}, f32[32,352]{1,0:T(8,128)S(1)}, ...) custom-call(s32[1,8]{1,0:T(1,128)S(1)} %bitcast.14, s32[64,1408]{1,0:T(8,128)S(1)} %bitcast.18, ...), custom_call_target="tpu_custom_call" | custom-call | flops 2000000000 | bytes 10000000 | tf_op jit(solution)/shard_map/first_flops/pallas_call | solution.py:218
  12.4 3.3 %all-to-all-done = f32[32,1,44]{2,1,0:T(1,128)S(1)} async-done(((f32[32,1,44]{2,1,0:T(1,128)}), f32[32,1,44]{2,1,0:T(1,128)S(1)}, u32[]{:S(2)}, u32[]{:S(2)}) %all-to-all-start) | async-done | bytes 5664 | tf_op jit(solution)/shard_map/all_to_all | solution.py:419
  15.8 0.6 %action_sums.1.grouped_ref.refs_0_ = f32[24,352]{1,0:T(8,128)S(1)} custom-call(f32[32,44]{1,0:T(8,128)S(1)} %bitcast.13, bf16[8,352,128]{2,1,0:T(8,128)(2,1)S(1)} %bitcast.12, bf16[24,128]{1,0:T(8,128)(2,1)S(1)} %get-tuple-element.14.weights_ref), custom_call_target="tpu_custom_call" | custom-call | flops 100000000 | bytes 1000000 | tf_op jit(solution)/shard_map/action_sums/pallas_call | solution.py:319
  16.4 0.6 %collective-permute-start.2 = (f32[24,352]{1,0:T(8,128)S(1)}, f32[24,352]{1,0:T(8,128)S(1)}, u32[]{:S(2)}, u32[]{:S(2)}) collective-permute-start(f32[24,352]{1,0:T(8,128)S(1)} %action_sums.1.grouped_ref.refs_0_), channel_id=1, source_target_pairs={{0,3},{1,2},{2,1},{3,0},{4,7},{5,6},{6,5},{7,4},{8,11},{9,10},{10,... | collective-permute-start | bytes 101384 | tf_op jit(solution)/shard_map/ppermute | solution.py:435
  16.9 1.4 %collective-permute-start.1 = (f32[24,352]{1,0:T(8,128)S(1)}, f32[24,352]{1,0:T(8,128)S(1)}, u32[]{:S(2)}, u32[]{:S(2)}) collective-permute-start(f32[24,352]{1,0:T(8,128)S(1)} %action_sums.1.grouped_ref.refs_0_), channel_id=1, source_target_pairs={{0,2},{1,3},{2,0},{3,1},{4,6},{5,7},{6,4},{7,5},{8,10},{9,11},{10,... | collective-permute-start | bytes 101384 | tf_op jit(solution)/shard_map/ppermute | solution.py:435
  18.4 2.4 %collective-permute-start = (f32[24,352]{1,0:T(8,128)S(1)}, f32[24,352]{1,0:T(8,128)S(1)}, u32[]{:S(2)}, u32[]{:S(2)}) collective-permute-start(f32[24,352]{1,0:T(8,128)S(1)} %action_sums.1.grouped_ref.refs_0_), channel_id=1, source_target_pairs={{0,1},{1,0},{2,3},{3,2},{4,5},{5,4},{6,7},{7,6},{8,9},{9,8},{10,11... | collective-permute-start | bytes 101384 | tf_op jit(solution)/shard_map/ppermute | solution.py:435
  20.8 2.9 %other_flops.1.sums_ref = bf16[8,1408,352]{2,1,0:T(8,128)(2,1)S(1)} custom-call(s32[1,8]{1,0:T(1,128)S(1)} %bitcast.15, f32[32,1408]{1,0:T(8,128)S(1)} %get-tuple-element.11.rank_rows, f32[32,352]{1,0:T(8,128)S(1)} %get-tuple-element.12.own_rows, bf16[1408,352]{1,0:T(8,128)(2,1)S(1)} %get-tuple-element.13.clear, ...), custom_call_target="tpu_custom_call" | custom-call | flops 2000000000 | bytes 10000000 | tf_op jit(solution)/shard_map/other_flops/pallas_call | solution.py:266
  23.8 0.0 collective-permute-done.2.refs_3_
  23.8 0.0 collective-permute-done.1.refs_2_
  23.8 0.0 collective-permute-done.refs_1_
  23.8 1.5 %best_response.1 = f32[1,384]{1,0:T(1,128)S(1)} custom-call(s32[1,8]{1,0:T(1,128)S(1)} %bitcast.16, s32[1,8]{1,0:T(1,128)S(1)} %bitcast.17, bf16[8,1408,352]{2,1,0:T(8,128)(2,1)S(1)} %other_flops.1.sums_ref, bf16[1408,352]{1,0:T(8,128)(2,1)S(1)} %get-tuple-element.16.near_ref, f32[24,352]{1,0:T(8,128)S(1)} %action_sums.1.grouped_ref.refs_0_, ...), custom_call_target="tpu_custom_call" | custom-call | flops 1000000000 | bytes 10000000 | tf_op jit(solution)/shard_map/best_response/pallas_call | solution.py:368
  25.3 0.1 collective-permute-start.3
  25.4 1.1 %collective-permute-done.3 = f32[1,384]{1,0:T(1,128)S(1)} collective-permute-done((f32[1,384]{1,0:T(1,128)S(1)}, f32[1,384]{1,0:T(1,128)S(1)}, u32[]{:S(2)}, u32[]{:S(2)}) %collective-permute-start.3) | collective-permute-done | bytes 1568 | tf_op jit(solution)/shard_map/ppermute | solution.py:400
  26.5 0.0 collective-permute-start.6
  26.5 1.3 %collective-permute-start.5 = (f32[1,384]{1,0:T(1,128)S(1)}, f32[1,384]{1,0:T(1,128)S(1)}, u32[]{:S(2)}, u32[]{:S(2)}) collective-permute-start(f32[1,384]{1,0:T(1,128)S(1)} %add.3.refs_0_), channel_id=1, source_target_pairs={{0,16},{4,20},{8,24},{12,28},{16,0},{20,4},{24,8},{28,12},{1,17},{... | collective-permute-start | bytes 4616 | tf_op jit(solution)/shard_map/ppermute | solution.py:400
  27.9 2.1 %collective-permute-start.4 = (f32[1,384]{1,0:T(1,128)S(1)}, f32[1,384]{1,0:T(1,128)S(1)}, u32[]{:S(2)}, u32[]{:S(2)}) collective-permute-start(f32[1,384]{1,0:T(1,128)S(1)} %add.3.refs_0_), channel_id=1, source_target_pairs={{0,8},{4,12},{8,0},{12,4},{16,24},{20,28},{24,16},{28,20},{1,9},{5... | collective-permute-start | bytes 4616 | tf_op jit(solution)/shard_map/ppermute | solution.py:400
  30.0 1.0 %collective-permute-done.6.refs_3_ = f32[1,384]{1,0:T(1,128)S(1)} collective-permute-done((f32[1,384]{1,0:T(1,128)S(1)}, f32[1,384]{1,0:T(1,128)S(1)}, u32[]{:S(2)}, u32[]{:S(2)}) %collective-permute-start.6) | collective-permute-done | bytes 1568 | tf_op jit(solution)/shard_map/ppermute | solution.py:400
  31.0 0.0 collective-permute-done.5.refs_2_
  31.0 0.6 %collective-permute-done.4.refs_1_ = f32[1,384]{1,0:T(1,128)S(1)} collective-permute-done((f32[1,384]{1,0:T(1,128)S(1)}, f32[1,384]{1,0:T(1,128)S(1)}, u32[]{:S(2)}, u32[]{:S(2)}) %collective-permute-start.4) | collective-permute-done | bytes 1568 | tf_op jit(solution)/shard_map/ppermute | solution.py:400
  31.6 0.6 %finish.1 = f32[352]{0:T(512)} custom-call(f32[1,384]{1,0:T(1,128)S(1)} %add.3.refs_0_, f32[1,384]{1,0:T(1,128)S(1)} %collective-permute-done.4.refs_1_, f32[1,384]{1,0:T(1,128)S(1)} %collective-permute-done.5.refs_2_, f32[1,384]{1,0:T(1,128)S(1)} %collective-permute-done.6.refs_3_), custom_call_target="tpu_custom_call" | custom-call | bytes 1000000 | tf_op jit(solution)/shard_map/finish/pallas_call | solution.py:388
  (9 shorter events, 0.0 us)
Async XLA Ops:
  0.0 0.7 %copy-start.5 = (f32[44]{0:T(128)S(1)}, f32[44]{0:T(128)}, u32[]{:S(2)}) copy-start(f32[44]{0:T(128)} %param.9) | copy-start | bytes 532
  0.7 8.0 %copy-start.1 = (s32[8]{0:T(128)S(1)}, s32[8]{0:T(128)}, u32[]{:S(2)}) copy-start(s32[8]{0:T(128)} %param.13) | copy-start | bytes 100
  0.7 8.0 %copy-start.3 = (s32[8,8,1408]{2,1,0:T(8,128)S(1)}, s32[8,8,1408]{2,1,0:T(8,128)}, u32[]{:S(2)}) copy-start(s32[8,8,1408]{2,1,0:T(8,128)} %param.11) | copy-start | bytes 1081348
  0.7 8.0 %copy-start.4 = (s32[8,8,5]{1,0,2:T(8,128)S(1)}, s32[8,8,5]{1,0,2:T(8,128)}, u32[]{:S(2)}) copy-start(s32[8,8,5]{1,0,2:T(8,128)} %param.12) | copy-start | bytes 3844
  0.7 8.0 %copy-start.6 = (f32[128]{0:T(128)S(1)}, f32[128]{0:T(128)}, u32[]{:S(2)}) copy-start(f32[128]{0:T(128)} %param.15) | copy-start | bytes 1540
  0.7 8.0 %copy-start.7 = (s32[128]{0:T(128)S(1)}, s32[128]{0:T(128)}, u32[]{:S(2)}) copy-start(s32[128]{0:T(128)} %param.16) | copy-start | bytes 1540
  0.7 8.0 %copy-start.8 = (s32[2,1408]{1,0:T(2,128)S(1)}, s32[2,1408]{1,0:T(2,128)}, u32[]{:S(2)}) copy-start(s32[2,1408]{1,0:T(2,128)} %constant.2.clone.cards_ref) | copy-start | bytes 33796
  0.7 15.1 %copy-start = (bf16[8,128,352]{1,2,0:T(8,128)(2,1)S(1)}, bf16[8,128,352]{1,2,0:T(8,128)(2,1)}, u32[]{:S(2)}) copy-start(bf16[8,128,352]{1,2,0:T(8,128)(2,1)} %param.10) | copy-start | bytes 2162692
  1.3 14.5 %all-to-all-start = ((f32[32,1,44]{2,1,0:T(1,128)}), f32[32,1,44]{2,1,0:T(1,128)S(1)}, u32[]{:S(2)}, u32[]{:S(2)}) async-start(f32[32,1,44]{2,1,0:T(1,128)} %bitcast.8), calls=%async_computation | async-start | bytes 32768 | tf_op jit(solution)/shard_map/all_to_all | solution.py:419
  16.4 7.4 %collective-permute-start.2 = (f32[24,352]{1,0:T(8,128)S(1)}, f32[24,352]{1,0:T(8,128)S(1)}, u32[]{:S(2)}, u32[]{:S(2)}) collective-permute-start(f32[24,352]{1,0:T(8,128)S(1)} %action_sums.1.grouped_ref.refs_0_), channel_id=1, source_target_pairs={{0,3},{1,2},{2,1},{3,0},{4,7},{5,6},{6,5},{7,4},{8,11},{9,10},{10,... | collective-permute-start | bytes 101384 | tf_op jit(solution)/shard_map/ppermute | solution.py:435
  16.9 6.8 %collective-permute-start.1 = (f32[24,352]{1,0:T(8,128)S(1)}, f32[24,352]{1,0:T(8,128)S(1)}, u32[]{:S(2)}, u32[]{:S(2)}) collective-permute-start(f32[24,352]{1,0:T(8,128)S(1)} %action_sums.1.grouped_ref.refs_0_), channel_id=1, source_target_pairs={{0,2},{1,3},{2,0},{3,1},{4,6},{5,7},{6,4},{7,5},{8,10},{9,11},{10,... | collective-permute-start | bytes 101384 | tf_op jit(solution)/shard_map/ppermute | solution.py:435
  18.4 5.4 %collective-permute-start = (f32[24,352]{1,0:T(8,128)S(1)}, f32[24,352]{1,0:T(8,128)S(1)}, u32[]{:S(2)}, u32[]{:S(2)}) collective-permute-start(f32[24,352]{1,0:T(8,128)S(1)} %action_sums.1.grouped_ref.refs_0_), channel_id=1, source_target_pairs={{0,1},{1,0},{2,3},{3,2},{4,5},{5,4},{6,7},{7,6},{8,9},{9,8},{10,11... | collective-permute-start | bytes 101384 | tf_op jit(solution)/shard_map/ppermute | solution.py:435
  20.8 3.0 %copy-start.2 = (s32[8]{0:T(128)S(1)}, s32[8]{0:T(128)}, u32[]{:S(2)}) copy-start(s32[8]{0:T(128)} %param.14) | copy-start | bytes 100
  25.3 1.2 %collective-permute-start.3 = (f32[1,384]{1,0:T(1,128)S(1)}, f32[1,384]{1,0:T(1,128)S(1)}, u32[]{:S(2)}, u32[]{:S(2)}) collective-permute-start(f32[1,384]{1,0:T(1,128)S(1)} %best_response.1), channel_id=1, source_target_pairs={{0,4},{4,0},{8,12},{12,8},{16,20},{20,16},{24,28},{28,24},{1,5},{5... | collective-permute-start | bytes 4616 | tf_op jit(solution)/shard_map/ppermute | solution.py:400
  26.5 4.5 %collective-permute-start.6 = (f32[1,384]{1,0:T(1,128)S(1)}, f32[1,384]{1,0:T(1,128)S(1)}, u32[]{:S(2)}, u32[]{:S(2)}) collective-permute-start(f32[1,384]{1,0:T(1,128)S(1)} %add.3.refs_0_), channel_id=1, source_target_pairs={{0,24},{4,28},{8,16},{12,20},{16,8},{20,12},{24,0},{28,4},{1,25},{... | collective-permute-start | bytes 4616 | tf_op jit(solution)/shard_map/ppermute | solution.py:400
  26.5 4.5 %collective-permute-start.5 = (f32[1,384]{1,0:T(1,128)S(1)}, f32[1,384]{1,0:T(1,128)S(1)}, u32[]{:S(2)}, u32[]{:S(2)}) collective-permute-start(f32[1,384]{1,0:T(1,128)S(1)} %add.3.refs_0_), channel_id=1, source_target_pairs={{0,16},{4,20},{8,24},{12,28},{16,0},{20,4},{24,8},{28,12},{1,17},{... | collective-permute-start | bytes 4616 | tf_op jit(solution)/shard_map/ppermute | solution.py:400
  27.9 3.7 %collective-permute-start.4 = (f32[1,384]{1,0:T(1,128)S(1)}, f32[1,384]{1,0:T(1,128)S(1)}, u32[]{:S(2)}, u32[]{:S(2)}) collective-permute-start(f32[1,384]{1,0:T(1,128)S(1)} %add.3.refs_0_), channel_id=1, source_target_pairs={{0,8},{4,12},{8,0},{12,4},{16,24},{20,28},{24,16},{28,20},{1,9},{5... | collective-permute-start | bytes 4616 | tf_op jit(solution)/shard_map/ppermute | solution.py:400
